TPU v7x, 128 devices: a whole 4x4x4 slice. The times are simulated.
128 devices in a mesh: head: 8 (over y_lo, x), vocab: 16 (over y_hi, z, core).
Axes of the slice: x: 4, y: 4 (y_hi: 2, y_lo: 2; y = y_hi * 2 + y_lo), z: 4, core: 2. Of those that a mesh axis runs over, the one named last changes fastest.
Arguments:
- hidden_rows: bfloat16 [512, 2048], P(('head', 'vocab')), may hold values from -240 to 240
- head_weight: bfloat16 [8, 2048, 32768], P('head', None, 'vocab'), may hold values from -0.125 to 0.125
- teacher_logits: bfloat16 [8, 512, 32768], P('head', 'vocab'), may hold values from -24 to 336
Outputs:
- weight_grad: bfloat16 [8, 2048, 32768], P('head', None, 'vocab')
- input_grad: float32 [512, 2048], P(('head', 'vocab'))
All inputs are finite; a program needn't handle non-finite values.
Results may differ from a plain program's by a relative error of at most 0.004.
Values may be sent and summed in bfloat16 or wider, within the bound.
A program may use at most 128 MiB of HBM per device.

v0:
```python
import jax
import jax.numpy as jnp
from jax import lax
from jax.sharding import PartitionSpec as P


def per_device(hidden_rows, head_weight, teacher_logits):
    trunk = lax.all_gather(hidden_rows, ("head", "vocab"), axis=0, tiled=True)
    weight = head_weight[0]
    teacher_tile = lax.all_to_all(teacher_logits, "vocab", split_axis=2, concat_axis=1, tiled=True)
    teacher = teacher_tile[0].astype(jnp.float32)
    student = jnp.dot(trunk, weight, preferred_element_type=jnp.float32)
    top_student, top_teacher = lax.pmax(
        (jnp.max(student, axis=1), jnp.max(teacher, axis=1)), "vocab"
    )
    student_exp = jnp.exp(student - top_student[:, None])
    teacher_exp = jnp.exp(teacher - top_teacher[:, None])
    total_student, total_teacher = lax.psum(
        (jnp.sum(student_exp, axis=1), jnp.sum(teacher_exp, axis=1)), "vocab"
    )
    student_prob = student_exp / total_student[:, None]
    teacher_prob = teacher_exp / total_teacher[:, None]
    logit_grad = (student_prob - teacher_prob).astype(jnp.bfloat16)
    weight_grad = lax.dot_general(
        trunk, logit_grad, (((0,), (0,)), ((), ())), preferred_element_type=jnp.float32
    )
    weight_grad = weight_grad.astype(jnp.bfloat16)[None]
    input_grad = lax.psum_scatter(
        lax.dot_general(
            logit_grad, weight, (((1,), (1,)), ((), ())), preferred_element_type=jnp.float32
        ),
        ("head", "vocab"),
        scatter_dimension=0,
        tiled=True,
    )
    return (weight_grad, input_grad)


def solution(mesh):
    return jax.shard_map(
        per_device,
        mesh=mesh,
        in_specs=(P(("head", "vocab"), None), P("head", None, "vocab"), P("head", "vocab", None)),
        out_specs=(P("head", None, "vocab"), P(("head", "vocab"), None)),
        check_vma=False,
    )
```

profile of v0, /device:TPU:1, one launch (start us, length us, event | category | flops | bytes accessed | tf_op | source)
XLA Modules:
  0.0 586.4 jit_solution(9616785559908552912)
XLA Ops:
  7.2 0.7 all-gather.3.cloned.1.call-update
  7.9 30.9 %copy.31 = bf16[1,32,32768]{1,0,2:T(2,128)(2,1)} copy(bf16[1,32,32768]{2,1,0:T(8,128)(2,1)} %param.5) | data formatting | bytes 4194304 | tf_op args[2]
  38.9 0.5 broadcast.7
  39.4 179.3 %reduce.3 = bf16[32768,32]{1,0:T(8,128)(2,1)} reduce(bf16[32768,1,32]{2,1,0:T(2,128)(2,1)} %bitcast.51, bf16[]{:T(256)} %broadcast.7), dimensions={1}, to_apply=%bitcast.39.reduce_sub_computation | reduce | bytes 4194306
  218.7 13.4 %reshape.25 = bf16[16,2,32768]{2,1,0:T(2,128)(2,1)S(1)} reshape(bf16[32768,32]{1,0:T(8,128)(2,1)} %reduce.3) | data formatting | bytes 4194304
  232.1 37.5 %all_to_all.15 = bf16[16,2,32768]{2,1,0:T(2,128)(2,1)} all-to-all(bf16[16,2,32768]{2,1,0:T(2,128)(2,1)S(1)} %reshape.25), channel_id=1, replica_groups=mesh['head'=8,'vocab'=16] {'vocab'}, dimensions={0} | all-to-all | bytes 4194304 | tf_op jit(solution)/shard_map/all_to_all | solution.py:10
  269.6 14.5 %reshape.26 = bf16[32768,1,32]{2,1,0:T(2,128)(2,1)} reshape(bf16[16,2,32768]{2,1,0:T(2,128)(2,1)} %all_to_all.15) | data formatting | bytes 4194304
  284.1 31.3 %copy.32 = bf16[1,32,32768]{2,1,0:T(8,128)(2,1)} copy(bf16[1,32,32768]{1,0,2:T(2,128)(2,1)} %bitcast.50) | data formatting | bytes 4194304 | tf_op jit(solution)/shard_map/all_to_all | solution.py:10
  315.5 2.7 copy.38
  318.2 0.3 fusion.9
  318.6 0.1 copy.34
  318.6 0.1 reshape.22
  318.7 0.5 fusion.10
  319.3 4.4 copy.33
  323.7 4.0 reshape.24
  327.7 10.4 %fusion.11 = (f32[512]{0:T(512)S(1)}, f32[512,2048]{1,0:T(8,128)}) fusion(bf16[512,2048]{1,0:T(8,128)(2,1)} %reshape.24, bf16[1,2048,2048]{2,1,0:T(8,128)(2,1)} %param.4), kind=kOutput, calls=%fused_computation.17 | convolution fusion | flops 4296015360 | bytes 14682112 | tf_op jit(solution)/shard_map/dot_general | solution.py:12
  338.1 33.7 %all-reduce.2 = (f32[512]{0:T(512)S(1)}, f32[512]{0:T(512)S(1)}) all-reduce(f32[512]{0:T(512)S(1)} %reshape.22, f32[512]{0:T(512)S(1)} %get-tuple-element.20), channel_id=1, replica_groups=mesh['head'=8,'vocab'=16] {'vocab'}, use_global_device_ids=true, to_apply=%region_5.0 | all-reduce | flops 1024 | bytes 8192 | tf_op jit(solution)/shard_map/pmax | solution.py:13
  371.8 0.1 sub.30
  371.9 0.1 copy.35
  371.9 0.8 exponential_reduce_fusion
  372.7 0.1 copy.36
  372.8 0.1 reduce_sum.22
  372.9 2.9 fusion.8
  375.8 34.2 %all-reduce.1 = (f32[512]{0:T(512)S(1)}, f32[512]{0:T(512)S(1)}) all-reduce(f32[512]{0:T(512)S(1)} %reduce_sum.22, f32[512]{0:T(512)S(1)} %fusion.8), channel_id=1, replica_groups=mesh['head'=8,'vocab'=16] {'vocab'}, use_global_device_ids=true, to_apply=%region_7.0 | all-reduce | flops 1024 | bytes 8192 | tf_op jit(solution)/shard_map/psum | solution.py:18
  410.1 4.3 fusion.7
  414.4 1.3 copy-done.1
  415.7 9.5 %fusion = f32[512,2048]{1,0:T(8,128)} fusion(bf16[512,2048]{1,0:T(8,128)(2,1)S(1)} %fusion.7, bf16[1,2048,2048]{2,1,0:T(8,128)(2,1)} %param.4), kind=kOutput, calls=%fused_computation | convolution fusion | flops 4294967296 | bytes 14680064 | tf_op jit(solution)/shard_map/dot_general | solution.py:29
  425.1 1.6 copy-done
  426.7 8.4 %convert_bitcast_fusion = bf16[1,2048,2048]{1,2,0:T(8,128)(2,1)} fusion(bf16[512,2048]{1,0:T(8,128)(2,1)} %copy-done.1, bf16[512,2048]{1,0:T(8,128)(2,1)S(1)} %copy-done), kind=kOutput, calls=%fused_computation.4 | convolution fusion | flops 4299161600 | bytes 12582912 | tf_op jit(solution)/shard_map/dot_general | solution.py:24
  435.1 12.3 %copy.37 = bf16[1,2048,2048]{2,1,0:T(8,128)(2,1)} copy(bf16[1,2048,2048]{1,2,0:T(8,128)(2,1)} %convert_bitcast_fusion) | data formatting | bytes 16777216
  447.4 130.7 %all-reduce.5.cloned.1.call-done = f32[512,2048]{1,0:T(8,128)} async-done(((f32[512,2048]{1,0:T(8,128)}), f32[512,2048]{1,0:T(8,128)}) %all-reduce.5.cloned.1.call-update) | async-done | bytes 4194320
  578.1 1.5 constant_dynamic-slice_fusion
  (6 shorter events, 0.1 us)
Async XLA Ops:
  7.2 316.6 %all-gather.3.cloned.1.call-start = ((), (), s32[]{:S(2)}) async-start(), calls=%async_computation.1 | async-start | bytes 2113536 | tf_op jit(solution)/shard_map/all_gather | solution.py:8
  7.9 570.2 %all-reduce.5.cloned.1.call-start = ((), (), s32[]{:S(2)}) async-start(), calls=%async_computation.2 | async-start | bytes 8388608
  414.3 1.3 copy-start.1
  425.1 1.6 copy-start
Sparse Core Ops, SparseCore 0:
  9.7 197.2 all-gather.2
  425.3 152.7 all-reduce.4
where the time goes:
time: 592 us; the launch traced here: 586 us
  other arithmetic  188 us (32%)
  waiting for transfers between devices  131 us (22%)
  local copies, waits for them, and re-layouts  119 us (20%)
  blocking collectives  105 us (18%)
  matrix products  28.3 us (5%)
  between operations  14.1 us (2%)
    unnamed x1, other arithmetic  179 us
    unnamed x3, waiting for transfers between devices  131 us
    unnamed x12, local copies, waits for them, and re-layouts  82.7 us
    all_to_all x1, blocking collectives, per_device(): lax.all_to_all(teacher_logits, 'vocab', split_axis=2, concat_axis=1, tile...  37.5 us
    psum x1, blocking collectives, per_device(): lax.psum((jnp.sum(student_exp, axis=1), jnp.sum(teacher_exp, axis=1)), 'v...  34.2 us
    pmax x1, blocking collectives, per_device(): lax.pmax((jnp.max(student, axis=1), jnp.max(teacher, axis=1)), 'vocab')  33.7 us
    all_to_all x1, local copies, waits for them, and re-layouts, per_device(): lax.all_to_all(teacher_logits, 'vocab', split_axis=2, concat_axis=1, tile...  31.3 us
  transfers between devices with their start and end apart: 2, of which 1 were waited for; matrix products, arithmetic and copies ran while one was open for 51% of the time, Pallas kernels for 0%

commit v1 on v0

v1 whole, which is shorter than its diff:
```python
import jax
import jax.numpy as jnp
from jax import lax
from jax.experimental import pallas as pl
from jax.experimental.pallas import tpu as pltpu
from jax.sharding import PartitionSpec as P

MESH = pl.DeviceIdType.MESH
F32, BF16 = jnp.float32, jnp.bfloat16
HEAD, VOC, CHIPS = 8, 16, 8
D, TOK, COLS = 2048, 512, 2048
ROWS = TOK // VOC
HR = TOK // HEAD
HALF = D // 2
CW = 256
NC = COLS // CW
DK = HALF // CW


def kernel(
    h_ref, w_hbm, t_hbm, wg_hbm, out_ref,
    w_v, t_v, tbuf, h32, st1, hs, hb, ht, e_v, te_v, lg_v, wg_v,
    col, tst_src, tstat, stx, sbuf, x0s, x0r, r1s, r1r, r2s, r2r, r3s, r3r,
    local_sem, wg_sem,
    s1, r1, sa, ra, stt, rtt, s2, r2, sf, rf, sst, rst, sx, rx, sr1, rr1, sr2, rr2, sr3, rr3,
):
    hd, vc = lax.axis_index("head"), lax.axis_index("vocab")
    chip = vc // 2
    core = vc - 2 * chip
    sib = 2 * chip + 1 - core

    def rows_of(index, count):
        return pl.ds(pl.multiple_of(index * count, count), count)

    def each(start, stop, body):
        def step(j, carry):
            body(j)
            return carry
        lax.fori_loop(start, stop, step, 0)

    def voc(j):
        return lax.rem(vc + j, VOC)

    def voc_from(j):
        return lax.rem(vc + VOC - j, VOC)

    def head(j):
        return lax.rem(hd + j, HEAD)

    def head_from(j):
        return lax.rem(hd + HEAD - j, HEAD)

    def remote(src, dst, send, recv, **to):
        return pltpu.make_async_remote_copy(
            src_ref=src, dst_ref=dst, send_sem=send, recv_sem=recv, device_id=to, device_id_type=MESH
        )

    w_copy = pltpu.make_async_copy(w_hbm, w_v, local_sem.at[0])
    t_copy = pltpu.make_async_copy(t_hbm, t_v, local_sem.at[1])
    own_tile = pltpu.make_async_copy(
        t_hbm.at[:, rows_of(vc, COLS)], tbuf.at[rows_of(vc, ROWS), :], local_sem.at[2]
    )
    t_copy.start()
    w_copy.start()
    own_tile.start()
    h32[0] = h_ref[:, :HALF].astype(F32)
    h32[1] = h_ref[:, HALF:].astype(F32)

    barrier = pltpu.get_barrier_semaphore()
    each(1, VOC, lambda j: pl.semaphore_signal(barrier, inc=1, device_id={"vocab": voc(j)}, device_id_type=MESH))
    each(1, HEAD, lambda j: pl.semaphore_signal(barrier, inc=1, device_id={"head": head(j)}, device_id_type=MESH))
    pl.semaphore_wait(barrier, VOC - 1 + HEAD - 1)

    def ag1(j, owner, to):
        return remote(h32.at[lax.rem(to, 2)], st1.at[owner], s1.at[j], r1.at[j], vocab=to)

    each(1, VOC, lambda j: ag1(j, vc, voc(j)).start())

    def a2a(j, owner, to):
        return remote(
            t_hbm.at[:, rows_of(to, COLS)], tbuf.at[rows_of(owner, ROWS), :], sa.at[j], ra.at[j], vocab=to
        )

    each(1, VOC, lambda j: a2a(j, vc, voc(j)).start())

    st1[vc] = h32[core]
    each(1, VOC, lambda j: ag1(j, voc_from(j), voc(j)).wait_recv())
    for i in range(VOC):
        hs[4 * i : 4 * i + 4, :] = st1[i]
    hb[core, rows_of(hd, HR), :] = hs[...].astype(BF16)

    def ag2(j, owner):
        block = hb.at[core, rows_of(owner, HR), :]
        return remote(block, block, s2.at[j], r2.at[j], head=head(j))

    def fwd(j, owner, side):
        block = hb.at[side, rows_of(owner, HR), :]
        return remote(block, block, sf.at[j], rf.at[j], vocab=sib)

    each(1, HEAD, lambda j: ag2(j, hd).start())
    fwd(0, hd, core).start()

    t_copy.wait()
    TW = 2048

    def top_step(i, top):
        x = t_v[:, pl.ds(pl.multiple_of(i * TW, TW), TW)].astype(F32)
        for k in range(TW // 128):
            top = jnp.maximum(top, x[:, k * 128 : (k + 1) * 128])
        return top

    top = lax.fori_loop(0, COLS * VOC // TW, top_step, jnp.full((ROWS, 128), -jnp.inf, F32))
    top = jnp.broadcast_to(jnp.max(top, axis=1, keepdims=True), (ROWS, 128))

    def sum_step(i, total):
        x = t_v[:, pl.ds(pl.multiple_of(i * TW, TW), TW)].astype(F32)
        for k in range(TW // 128):
            total = total + jnp.exp(x[:, k * 128 : (k + 1) * 128] - top)
        return total

    total = lax.fori_loop(0, COLS * VOC // TW, sum_step, jnp.zeros((ROWS, 128), F32))
    scale = 1.0 / jnp.broadcast_to(jnp.sum(total, axis=1, keepdims=True), (ROWS, 128))
    lane = lax.broadcasted_iota(jnp.int32, (ROWS, 128), 1)
    both = jnp.where(lane < 64, top, scale)
    tst_src[...] = both
    tstat[rows_of(vc, ROWS), :] = both

    def tst(j, owner):
        return remote(tst_src, tstat.at[rows_of(owner, ROWS), :], stt.at[j], rtt.at[j], vocab=voc(j))

    each(1, VOC, lambda j: tst(j, vc).start())

    def pass_on(j):
        ag2(j, head_from(j)).wait_recv()
        fwd(j, head_from(j), core).start()

    each(1, HEAD, pass_on)
    fwd(0, hd, 1 - core).wait_recv()
    each(1, HEAD, lambda j: fwd(j, head_from(j), 1 - core).wait_recv())
    w_copy.wait()

    col[0] = jnp.full((TOK, 128), -jnp.inf, F32)

    def student_step(n):
        cols = pl.ds(pl.multiple_of(n * CW, CW), CW)
        x = jnp.dot(hb[0], w_v[:HALF, cols], preferred_element_type=F32)
        x = x + jnp.dot(hb[1], w_v[HALF:, cols], preferred_element_type=F32)
        e_v[n] = x
        col[0] = jnp.maximum(col[0], jnp.maximum(x[:, :128], x[:, 128:]))

    each(0, NC, student_step)
    col[0] = jnp.broadcast_to(jnp.max(col[0], axis=1, keepdims=True), (TOK, 128))
    col[1] = jnp.zeros((TOK, 128), F32)

    def exp_step(n):
        top_n = col[0]
        a = jnp.exp(e_v[n, :, :128] - top_n)
        b = jnp.exp(e_v[n, :, 128:] - top_n)
        e_v[n, :, :128] = a
        e_v[n, :, 128:] = b
        col[1] = col[1] + (a + b)

    each(0, NC, exp_step)
    sums = jnp.broadcast_to(jnp.sum(col[1], axis=1, keepdims=True), (TOK, 128))
    lane_t = lax.broadcasted_iota(jnp.int32, (TOK, 128), 1)
    stats = jnp.where(lane_t == 0, col[0], sums).T[:8, :]
    stx[...] = stats
    sbuf[vc] = stats

    def st(j, owner):
        return remote(stx, sbuf.at[owner], sst.at[j], rst.at[j], vocab=voc(j))

    each(1, VOC, lambda j: st(j, vc).start())

    for half in range(2):
        for k in range(DK):
            ht[half * HALF + k * CW : half * HALF + (k + 1) * CW, :] = hb[half, :, k * CW : (k + 1) * CW].T

    own_tile.wait()
    each(1, VOC, lambda j: tst(j, voc_from(j)).wait_recv())
    each(1, VOC, lambda j: a2a(j, voc_from(j), voc(j)).wait_recv())
    col[0] = jnp.broadcast_to(tstat[:, 0:1], (TOK, 128))
    col[1] = jnp.broadcast_to(tstat[:, 64:65], (TOK, 128))

    def teacher_step(n):
        for side in range(2):
            cols = pl.ds(pl.multiple_of(n * CW + side * 128, 128), 128)
            x = tbuf[:, cols].astype(F32)
            te_v[n, :, side * 128 : side * 128 + 128] = jnp.exp(x - col[0]) * col[1]

    each(0, NC, teacher_step)

    each(1, VOC, lambda j: st(j, voc_from(j)).wait_recv())
    tops = [sbuf[i][0:1, :] for i in range(VOC)]
    parts = [sbuf[i][1:2, :] for i in range(VOC)]
    top_all = tops[0]
    for x in tops[1:]:
        top_all = jnp.maximum(top_all, x)
    total_all = jnp.zeros_like(top_all)
    for x, y in zip(tops, parts):
        total_all = total_all + y * jnp.exp(x - top_all)
    factor = jnp.exp(stx[0:1, :] - top_all) / total_all
    col[0] = jnp.broadcast_to(factor, (128, TOK)).T

    def grad_step(n):
        for side in range(2):
            cols = pl.ds(pl.multiple_of(n * CW + side * 128, 128), 128)
            lanes = slice(side * 128, side * 128 + 128)
            lg_v[:, cols] = (e_v[n, :, lanes] * col[0] - te_v[n, :, lanes]).astype(BF16)

    each(0, NC, grad_step)

    def share(half, k):
        rows = pl.ds(pl.multiple_of(half * HALF + k * CW, CW), CW)
        return lax.dot_general(
            lg_v[...], w_v[rows, :], (((1,), (1,)), ((), ())), preferred_element_type=F32
        )

    def x0(k):
        return remote(x0s.at[k], x0r.at[k], sx.at[k], rx.at[k], vocab=sib)

    def give_step(k):
        x0s[k] = share(1 - core, k).astype(BF16)
        x0(k).start()

    each(0, DK, give_step)

    def rs1(k, j, to, owner):
        return remote(
            r1s.at[k, to], r1r.at[k, owner], sr1.at[k * HEAD + j], rr1.at[k * HEAD + j], head=head(j)
        )

    def keep_step(k):
        mine = share(core, k)
        x0(k).wait_recv()
        r1s[k] = (mine + x0r[k].astype(F32)).astype(BF16).reshape(HEAD, HR, CW)
        each(1, HEAD, lambda j: rs1(k, j, head(j), hd).start())
        r1r[k, hd] = r1s[k, hd]

    each(0, DK, keep_step)

    def wg_out(n):
        rows = pl.ds(pl.multiple_of(n * CW, CW), CW)
        return pltpu.make_async_copy(wg_v.at[rows, :], wg_hbm.at[rows, :], wg_sem.at[n])

    def weight_step(n):
        rows = pl.ds(pl.multiple_of(n * CW, CW), CW)
        wg_v[rows, :] = jnp.dot(ht[rows, :], lg_v[...], preferred_element_type=F32).astype(BF16)
        wg_out(n).start()

    each(0, D // CW, weight_step)

    for k in range(DK):
        each(1, HEAD, lambda j: rs1(k, j, head(j), head_from(j)).wait_recv())
        total = r1r[k, 0].astype(F32)
        for i in range(1, HEAD):
            total = total + r1r[k, i].astype(F32)
        r2s[:, :, k * CW : (k + 1) * CW] = total.reshape(CHIPS, 8, CW)

    def rs2(j, to, owner):
        return remote(r2s.at[to], r2r.at[owner], sr2.at[j], rr2.at[j], vocab=2 * to + core)

    def chip_at(j):
        return lax.rem(chip + j, CHIPS)

    each(1, CHIPS, lambda j: rs2(j, chip_at(j), chip).start())
    r2r[chip] = r2s[chip]
    each(1, CHIPS, lambda j: rs2(j, chip_at(j), lax.rem(chip + CHIPS - j, CHIPS)).wait_recv())
    mine = r2r[0]
    for i in range(1, CHIPS):
        mine = mine + r2r[i]
    r3s[...] = mine
    rs3 = remote(r3s, r3r, sr3, rr3, vocab=sib)
    rs3.start()
    rs3.wait_recv()
    other = r3r[...]
    first = core == 0
    low = jnp.where(first, mine, other)
    high = jnp.where(first, other, mine)
    out_ref[:, :HALF] = jnp.where(first, low[:4], low[4:])
    out_ref[:, HALF:] = jnp.where(first, high[:4], high[4:])

    each(1, VOC, lambda j: ag1(j, vc, voc(j)).wait_send())
    each(1, VOC, lambda j: a2a(j, vc, voc(j)).wait_send())
    each(1, VOC, lambda j: tst(j, vc).wait_send())
    each(1, VOC, lambda j: st(j, vc).wait_send())
    each(1, HEAD, lambda j: ag2(j, hd).wait_send())
    each(0, HEAD, lambda j: fwd(j, head_from(j), core).wait_send())
    each(0, DK, lambda k: x0(k).wait_send())
    for k in range(DK):
        each(1, HEAD, lambda j: rs1(k, j, head(j), hd).wait_send())
    each(1, CHIPS, lambda j: rs2(j, chip_at(j), chip).wait_send())
    rs3.wait_send()
    each(0, D // CW, lambda n: wg_out(n).wait())


def per_device(hidden_rows, head_weight, teacher_logits):
    hbm = pl.BlockSpec(memory_space=pltpu.MemorySpace.HBM)
    vmem = pl.BlockSpec(memory_space=pltpu.VMEM)
    dma = pltpu.SemaphoreType.DMA
    weight_grad, input_grad = pl.pallas_call(
        kernel,
        out_shape=(
            jax.ShapeDtypeStruct((D, COLS), BF16),
            jax.ShapeDtypeStruct((TOK // (HEAD * VOC), D), F32),
        ),
        in_specs=[vmem, hbm, hbm],
        out_specs=(hbm, vmem),
        scratch_shapes=[
            pltpu.VMEM((D, COLS), BF16),
            pltpu.VMEM((ROWS, COLS * VOC), BF16),
            pltpu.VMEM((TOK, COLS), BF16),
            pltpu.VMEM((2, 4, HALF), F32),
            pltpu.VMEM((VOC, 4, HALF), F32),
            pltpu.VMEM((HR, HALF), F32),
            pltpu.VMEM((2, TOK, HALF), BF16),
            pltpu.VMEM((D, TOK), BF16),
            pltpu.VMEM((NC, TOK, CW), F32),
            pltpu.VMEM((NC, TOK, CW), F32),
            pltpu.VMEM((TOK, COLS), BF16),
            pltpu.VMEM((D, COLS), BF16),
            pltpu.VMEM((2, TOK, 128), F32),
            pltpu.VMEM((ROWS, 128), F32),
            pltpu.VMEM((TOK, 128), F32),
            pltpu.VMEM((8, TOK), F32),
            pltpu.VMEM((VOC, 8, TOK), F32),
            pltpu.VMEM((DK, TOK, CW), BF16),
            pltpu.VMEM((DK, TOK, CW), BF16),
            pltpu.VMEM((DK, HEAD, HR, CW), BF16),
            pltpu.VMEM((DK, HEAD, HR, CW), BF16),
            pltpu.VMEM((CHIPS, 8, HALF), F32),
            pltpu.VMEM((CHIPS, 8, HALF), F32),
            pltpu.VMEM((8, HALF), F32),
            pltpu.VMEM((8, HALF), F32),
            dma((3,)), dma((D // CW,)),
            dma((VOC,)), dma((VOC,)), dma((VOC,)), dma((VOC,)), dma((VOC,)), dma((VOC,)),
            dma((HEAD,)), dma((HEAD,)), dma((HEAD,)), dma((HEAD,)),
            dma((VOC,)), dma((VOC,)), dma((DK,)), dma((DK,)),
            dma((DK * HEAD,)), dma((DK * HEAD,)), dma((CHIPS,)), dma((CHIPS,)), dma, dma,
        ],
        compiler_params=pltpu.CompilerParams(
            collective_id=0, has_side_effects=True, vmem_limit_bytes=56 * 1024 * 1024
        ),
        cost_estimate=pl.CostEstimate(
            flops=6 * TOK * D * COLS, bytes_accessed=20 * 1024 * 1024, transcendentals=3 * TOK * COLS
        ),
    )(hidden_rows, head_weight[0], teacher_logits[0])
    return weight_grad[None], input_grad


def solution(mesh):
    return jax.shard_map(
        per_device,
        mesh=mesh,
        in_specs=(P(("head", "vocab"), None), P("head", None, "vocab"), P("head", "vocab", None)),
        out_specs=(P("head", None, "vocab"), P(("head", "vocab"), None)),
        check_vma=False,
    )
```

time: 592 us -> 108 us (0.18)
  other arithmetic: 188 us -> 0 us
  waiting for transfers between devices: 131 us -> 0 us
  local copies, waits for them, and re-layouts: 119 us -> 9.07 us
  blocking collectives: 105 us -> 0 us
  Pallas kernels: 0 us -> 98.1 us
  matrix products: 28.3 us -> 0 us
  between operations: 14.1 us -> 0.65 us
    unnamed x1 -> x0, other arithmetic: 179 us -> none
    unnamed x3 -> x0, waiting for transfers between devices: 131 us -> none
    pallas_call x0 -> x1, Pallas kernels: none -> 98.1 us  [per_device(): pl.pallas_call(kernel, out_shape=(jax.ShapeDtypeStruct((D, COLS), BF16),...]
    unnamed x12 -> x4, local copies, waits for them, and re-layouts: 82.7 us -> 9.07 us
    all_to_all x1 -> x0, blocking collectives: 37.5 us -> none  [per_device(): lax.all_to_all(teacher_logits, 'vocab', split_axis=2, concat_axis=1, tile...]
    psum x1 -> x0, blocking collectives: 34.2 us -> none  [per_device(): lax.psum((jnp.sum(student_exp, axis=1), jnp.sum(teacher_exp, axis=1)), 'v...]
    pmax x1 -> x0, blocking collectives: 33.7 us -> none  [per_device(): lax.pmax((jnp.max(student, axis=1), jnp.max(teacher, axis=1)), 'vocab')]
    all_to_all x1 -> x0, local copies, waits for them, and re-layouts: 31.3 us -> none  [per_device(): lax.all_to_all(teacher_logits, 'vocab', split_axis=2, concat_axis=1, tile...]
  transfers between devices with their start and end apart: 2 -> 0, of which waited for: 1 -> 0; matrix products, arithmetic and copies ran while one was open for 51% -> 0% of each run, Pallas kernels for 0% -> 0%
where the time goes in v1:
time: 108 us
  Pallas kernels  98.1 us (91%)
  local copies, waits for them, and re-layouts  9.07 us (8%)
    pallas_call x1, Pallas kernels, per_device(): pl.pallas_call(kernel, out_shape=(jax.ShapeDtypeStruct((D, COLS), BF16),...  98.1 us
    unnamed x4, local copies, waits for them, and re-layouts  9.07 us

profile of v1, /device:TPU:1, one launch (start us, length us, event | category | flops | bytes accessed | tf_op | source)
XLA Modules:
  0.0 107.8 jit_solution(2445324357287496845)
XLA Ops:
  0.6 98.1 %shard_map.50 = (bf16[2048,2048]{1,0:T(8,128)(2,1)}, f32[4,2048]{1,0:T(4,128)}) custom-call(bf16[4,2048]{1,0:T(4,128)(2,1)} %h_ref.1, bf16[2048,2048]{1,0:T(8,128)(2,1)} %bitcast.4, bf16[32,32768]{1,0:T(8,128)(2,1)} %bitcast.5), custom_call_target="tpu_custom_call" | custom-call | flops 12884901888 | bytes 20971520 | tf_op jit(solution)/shard_map/pallas_call | solution.py:301
  98.7 0.0 copy-start
  98.7 8.4 %copy.7 = bf16[1,2048,2048]{2,1,0:T(8,128)(2,1)} copy(bf16[1,2048,2048]{2,1,0:T(8,128)(2,1)} %bitcast.3) | data formatting | bytes 16777216
  107.2 0.0 copy-done
  107.2 0.6 copy.8
Async XLA Ops:
  98.7 8.5 %copy-start = (f32[4,2048]{1,0:T(4,128)S(1)}, f32[4,2048]{1,0:T(4,128)}, u32[]{:S(2)}) copy-start(f32[4,2048]{1,0:T(4,128)} %get-tuple-element.9) | copy-start | bytes 98308

commit v2 on v1

--- a/solution.py
+++ b/solution.py
@@ -18,10 +18,10 @@
 
 
 def kernel(
-    h_ref, w_hbm, t_hbm, wg_hbm, out_ref,
-    w_v, t_v, tbuf, h32, st1, hs, hb, ht, e_v, te_v, lg_v, wg_v,
+    h_ref, w_hbm, t_hbm, wg_v, out_ref,
+    w_v, t_v, tbuf, pack, own, st1, hs, hb, ht, e_v, lg_v,
     col, tst_src, tstat, stx, sbuf, x0s, x0r, r1s, r1r, r2s, r2r, r3s, r3r,
-    local_sem, wg_sem,
+    local_sem,
     s1, r1, sa, ra, stt, rtt, s2, r2, sf, rf, sst, rst, sx, rx, sr1, rr1, sr2, rr2, sr3, rr3,
 ):
     hd, vc = lax.axis_index("head"), lax.axis_index("vocab")
@@ -63,8 +63,11 @@
     t_copy.start()
     w_copy.start()
     own_tile.start()
-    h32[0] = h_ref[:, :HALF].astype(F32)
-    h32[1] = h_ref[:, HALF:].astype(F32)
+    for side in range(2):
+        for g in range(4):
+            at = side * HALF + g * CW
+            pack[4 * g : 4 * g + 4, :] = h_ref[:, at : at + CW].astype(F32)
+        own[side] = pack[...].astype(BF16)
 
     barrier = pltpu.get_barrier_semaphore()
     each(1, VOC, lambda j: pl.semaphore_signal(barrier, inc=1, device_id={"vocab": voc(j)}, device_id_type=MESH))
@@ -72,33 +75,63 @@
     pl.semaphore_wait(barrier, VOC - 1 + HEAD - 1)
 
     def ag1(j, owner, to):
-        return remote(h32.at[lax.rem(to, 2)], st1.at[owner], s1.at[j], r1.at[j], vocab=to)
+        return remote(own.at[lax.rem(to, 2)], st1.at[owner], s1.at[j], r1.at[j], vocab=to)
 
     each(1, VOC, lambda j: ag1(j, vc, voc(j)).start())
+
+    y_hi = vc // 8
+
+    def tile_to(j):
+        near = lax.rem(vc + j, 8)
+        return 8 * lax.rem(y_hi + j // 8, 2) + near
+
+    def tile_from(j):
+        near = lax.rem(vc + 16 - j, 8)
+        return 8 * lax.rem(y_hi + j // 8, 2) + near
 
     def a2a(j, owner, to):
         return remote(
             t_hbm.at[:, rows_of(to, COLS)], tbuf.at[rows_of(owner, ROWS), :], sa.at[j], ra.at[j], vocab=to
         )
 
-    each(1, VOC, lambda j: a2a(j, vc, voc(j)).start())
-
-    st1[vc] = h32[core]
+    each(1, 8, lambda j: a2a(j, vc, tile_to(j)).start())
+
+    st1[vc] = own[core]
     each(1, VOC, lambda j: ag1(j, voc_from(j), voc(j)).wait_recv())
     for i in range(VOC):
-        hs[4 * i : 4 * i + 4, :] = st1[i]
+        rows = st1[i].astype(F32)
+        for g in range(4):
+            hs[4 * i : 4 * i + 4, g * CW : (g + 1) * CW] = rows[4 * g : 4 * g + 4, :]
     hb[core, rows_of(hd, HR), :] = hs[...].astype(BF16)
 
-    def ag2(j, owner):
-        block = hb.at[core, rows_of(owner, HR), :]
-        return remote(block, block, s2.at[j], r2.at[j], head=head(j))
-
-    def fwd(j, owner, side):
-        block = hb.at[side, rows_of(owner, HR), :]
-        return remote(block, block, sf.at[j], rf.at[j], vocab=sib)
-
-    each(1, HEAD, lambda j: ag2(j, hd).start())
-    fwd(0, hd, core).start()
+    y_lo = hd // 4
+    x_at = hd - 4 * y_lo
+
+    def head_at(p, j):
+        return 4 * lax.rem(y_lo + p, 2) + lax.rem(x_at + 4 + j, 4)
+
+    def block(side, p, j):
+        return hb.at[side, rows_of(head_at(p, j), HR), :]
+
+    def agy(p):
+        return remote(block(core, p, 0), block(core, p, 0), s2.at[0], r2.at[0], head=head_at(1, 0))
+
+    def agx(p, j, src):
+        return remote(
+            block(core, p, src), block(core, p, src), s2.at[4 * p + j], r2.at[4 * p + j], head=head_at(0, j)
+        )
+
+    def fwd(p, j, side):
+        at = block(side, p, -j)
+        return remote(at, at, sf.at[4 * p + j], rf.at[4 * p + j], vocab=sib)
+
+    agy(0).start()
+    each(1, 4, lambda j: agx(0, j, 0).start())
+    fwd(0, 0, core).start()
+    each(8, VOC, lambda j: a2a(j, vc, tile_to(j)).start())
+    agy(1).wait_recv()
+    each(1, 4, lambda j: agx(1, j, 0).start())
+    fwd(1, 0, core).start()
 
     t_copy.wait()
     TW = 2048
@@ -121,22 +154,23 @@
     total = lax.fori_loop(0, COLS * VOC // TW, sum_step, jnp.zeros((ROWS, 128), F32))
     scale = 1.0 / jnp.broadcast_to(jnp.sum(total, axis=1, keepdims=True), (ROWS, 128))
     lane = lax.broadcasted_iota(jnp.int32, (ROWS, 128), 1)
-    both = jnp.where(lane < 64, top, scale)
-    tst_src[...] = both
-    tstat[rows_of(vc, ROWS), :] = both
+    both = jnp.concatenate([jnp.where(lane == 0, top, scale), jnp.zeros((128 - ROWS, 128), F32)])
+    tst_src[...] = both.T[:8]
+    tstat[vc] = tst_src[...]
 
     def tst(j, owner):
-        return remote(tst_src, tstat.at[rows_of(owner, ROWS), :], stt.at[j], rtt.at[j], vocab=voc(j))
+        return remote(tst_src, tstat.at[owner], stt.at[j], rtt.at[j], vocab=voc(j))
 
     each(1, VOC, lambda j: tst(j, vc).start())
 
-    def pass_on(j):
-        ag2(j, head_from(j)).wait_recv()
-        fwd(j, head_from(j), core).start()
-
-    each(1, HEAD, pass_on)
-    fwd(0, hd, 1 - core).wait_recv()
-    each(1, HEAD, lambda j: fwd(j, head_from(j), 1 - core).wait_recv())
+    for p in range(2):
+        def pass_on(j):
+            agx(p, j, -j).wait_recv()
+            fwd(p, j, core).start()
+
+        each(1, 4, pass_on)
+    for p in range(2):
+        each(0, 4, lambda j: fwd(p, j, 1 - core).wait_recv())
     w_copy.wait()
 
     col[0] = jnp.full((TOK, 128), -jnp.inf, F32)
@@ -164,8 +198,10 @@
     sums = jnp.broadcast_to(jnp.sum(col[1], axis=1, keepdims=True), (TOK, 128))
     lane_t = lax.broadcasted_iota(jnp.int32, (TOK, 128), 1)
     stats = jnp.where(lane_t == 0, col[0], sums).T[:8, :]
-    stx[...] = stats
-    sbuf[vc] = stats
+    for i in range(4):
+        stx[i : i + 1, :] = stats[0:1, i * 128 : (i + 1) * 128]
+        stx[4 + i : 5 + i, :] = stats[1:2, i * 128 : (i + 1) * 128]
+    sbuf[vc] = stx[...]
 
     def st(j, owner):
         return remote(stx, sbuf.at[owner], sst.at[j], rst.at[j], vocab=voc(j))
@@ -176,37 +212,35 @@
         for k in range(DK):
             ht[half * HALF + k * CW : half * HALF + (k + 1) * CW, :] = hb[half, :, k * CW : (k + 1) * CW].T
 
-    own_tile.wait()
     each(1, VOC, lambda j: tst(j, voc_from(j)).wait_recv())
-    each(1, VOC, lambda j: a2a(j, voc_from(j), voc(j)).wait_recv())
-    col[0] = jnp.broadcast_to(tstat[:, 0:1], (TOK, 128))
-    col[1] = jnp.broadcast_to(tstat[:, 64:65], (TOK, 128))
-
-    def teacher_step(n):
-        for side in range(2):
-            cols = pl.ds(pl.multiple_of(n * CW + side * 128, 128), 128)
-            x = tbuf[:, cols].astype(F32)
-            te_v[n, :, side * 128 : side * 128 + 128] = jnp.exp(x - col[0]) * col[1]
-
-    each(0, NC, teacher_step)
+    for i in range(4):
+        rows = jnp.concatenate([tstat[4 * i + k][:, :ROWS] for k in range(4)], axis=1)
+        rows = jnp.concatenate([rows, jnp.zeros((120, 128), F32)]).T
+        col[0, i * 128 : (i + 1) * 128, :] = jnp.broadcast_to(rows[:, 0:1], (128, 128))
+        col[1, i * 128 : (i + 1) * 128, :] = jnp.broadcast_to(rows[:, 1:2], (128, 128))
 
     each(1, VOC, lambda j: st(j, voc_from(j)).wait_recv())
-    tops = [sbuf[i][0:1, :] for i in range(VOC)]
-    parts = [sbuf[i][1:2, :] for i in range(VOC)]
+    tops = [sbuf[i][:4] for i in range(VOC)]
+    parts = [sbuf[i][4:] for i in range(VOC)]
     top_all = tops[0]
     for x in tops[1:]:
         top_all = jnp.maximum(top_all, x)
     total_all = jnp.zeros_like(top_all)
     for x, y in zip(tops, parts):
         total_all = total_all + y * jnp.exp(x - top_all)
-    factor = jnp.exp(stx[0:1, :] - top_all) / total_all
-    col[0] = jnp.broadcast_to(factor, (128, TOK)).T
+    factor = jnp.exp(stx[:4] - top_all) / total_all
+    for i in range(4):
+        col[2, i * 128 : (i + 1) * 128, :] = jnp.broadcast_to(factor[i : i + 1], (128, 128)).T
+
+    own_tile.wait()
+    each(1, VOC, lambda j: a2a(j, tile_from(j), tile_to(j)).wait_recv())
 
     def grad_step(n):
         for side in range(2):
             cols = pl.ds(pl.multiple_of(n * CW + side * 128, 128), 128)
-            lanes = slice(side * 128, side * 128 + 128)
-            lg_v[:, cols] = (e_v[n, :, lanes] * col[0] - te_v[n, :, lanes]).astype(BF16)
+            teacher = jnp.exp(tbuf[:, cols].astype(F32) - col[0]) * col[1]
+            student = e_v[n, :, side * 128 : side * 128 + 128] * col[2]
+            lg_v[:, cols] = (student - teacher).astype(BF16)
 
     each(0, NC, grad_step)
 
@@ -239,14 +273,9 @@
 
     each(0, DK, keep_step)
 
-    def wg_out(n):
-        rows = pl.ds(pl.multiple_of(n * CW, CW), CW)
-        return pltpu.make_async_copy(wg_v.at[rows, :], wg_hbm.at[rows, :], wg_sem.at[n])
-
     def weight_step(n):
         rows = pl.ds(pl.multiple_of(n * CW, CW), CW)
         wg_v[rows, :] = jnp.dot(ht[rows, :], lg_v[...], preferred_element_type=F32).astype(BF16)
-        wg_out(n).start()
 
     each(0, D // CW, weight_step)
 
@@ -281,17 +310,18 @@
     out_ref[:, HALF:] = jnp.where(first, high[:4], high[4:])
 
     each(1, VOC, lambda j: ag1(j, vc, voc(j)).wait_send())
-    each(1, VOC, lambda j: a2a(j, vc, voc(j)).wait_send())
+    each(1, VOC, lambda j: a2a(j, vc, tile_to(j)).wait_send())
     each(1, VOC, lambda j: tst(j, vc).wait_send())
     each(1, VOC, lambda j: st(j, vc).wait_send())
-    each(1, HEAD, lambda j: ag2(j, hd).wait_send())
-    each(0, HEAD, lambda j: fwd(j, head_from(j), core).wait_send())
+    agy(0).wait_send()
+    for p in range(2):
+        each(1, 4, lambda j: agx(p, j, 0).wait_send())
+        each(0, 4, lambda j: fwd(p, j, core).wait_send())
     each(0, DK, lambda k: x0(k).wait_send())
     for k in range(DK):
         each(1, HEAD, lambda j: rs1(k, j, head(j), hd).wait_send())
     each(1, CHIPS, lambda j: rs2(j, chip_at(j), chip).wait_send())
     rs3.wait_send()
-    each(0, D // CW, lambda n: wg_out(n).wait())
 
 
 def per_device(hidden_rows, head_weight, teacher_logits):
@@ -301,29 +331,28 @@
     weight_grad, input_grad = pl.pallas_call(
         kernel,
         out_shape=(
-            jax.ShapeDtypeStruct((D, COLS), BF16),
+            pltpu.VMEM((D, COLS), BF16),
             jax.ShapeDtypeStruct((TOK // (HEAD * VOC), D), F32),
         ),
         in_specs=[vmem, hbm, hbm],
-        out_specs=(hbm, vmem),
+        out_specs=(vmem, vmem),
         scratch_shapes=[
             pltpu.VMEM((D, COLS), BF16),
             pltpu.VMEM((ROWS, COLS * VOC), BF16),
             pltpu.VMEM((TOK, COLS), BF16),
-            pltpu.VMEM((2, 4, HALF), F32),
-            pltpu.VMEM((VOC, 4, HALF), F32),
+            pltpu.VMEM((16, CW), F32),
+            pltpu.VMEM((2, 16, CW), BF16),
+            pltpu.VMEM((VOC, 16, CW), BF16),
             pltpu.VMEM((HR, HALF), F32),
             pltpu.VMEM((2, TOK, HALF), BF16),
             pltpu.VMEM((D, TOK), BF16),
             pltpu.VMEM((NC, TOK, CW), F32),
-            pltpu.VMEM((NC, TOK, CW), F32),
             pltpu.VMEM((TOK, COLS), BF16),
-            pltpu.VMEM((D, COLS), BF16),
-            pltpu.VMEM((2, TOK, 128), F32),
-            pltpu.VMEM((ROWS, 128), F32),
-            pltpu.VMEM((TOK, 128), F32),
-            pltpu.VMEM((8, TOK), F32),
-            pltpu.VMEM((VOC, 8, TOK), F32),
+            pltpu.VMEM((3, TOK, 128), F32),
+            pltpu.VMEM((8, 128), F32),
+            pltpu.VMEM((VOC, 8, 128), F32),
+            pltpu.VMEM((8, 128), F32),
+            pltpu.VMEM((VOC, 8, 128), F32),
             pltpu.VMEM((DK, TOK, CW), BF16),
             pltpu.VMEM((DK, TOK, CW), BF16),
             pltpu.VMEM((DK, HEAD, HR, CW), BF16),
@@ -332,14 +361,14 @@
             pltpu.VMEM((CHIPS, 8, HALF), F32),
             pltpu.VMEM((8, HALF), F32),
             pltpu.VMEM((8, HALF), F32),
-            dma((3,)), dma((D // CW,)),
+            dma((3,)),
             dma((VOC,)), dma((VOC,)), dma((VOC,)), dma((VOC,)), dma((VOC,)), dma((VOC,)),
             dma((HEAD,)), dma((HEAD,)), dma((HEAD,)), dma((HEAD,)),
             dma((VOC,)), dma((VOC,)), dma((DK,)), dma((DK,)),
             dma((DK * HEAD,)), dma((DK * HEAD,)), dma((CHIPS,)), dma((CHIPS,)), dma, dma,
         ],
         compiler_params=pltpu.CompilerParams(
-            collective_id=0, has_side_effects=True, vmem_limit_bytes=56 * 1024 * 1024
+            collective_id=0, has_side_effects=True, vmem_limit_bytes=44 * 1024 * 1024
         ),
         cost_estimate=pl.CostEstimate(
             flops=6 * TOK * D * COLS, bytes_accessed=20 * 1024 * 1024, transcendentals=3 * TOK * COLS

time: 108 us -> 79.6 us (0.74)
  Pallas kernels: 98.1 us -> 74.1 us
  local copies, waits for them, and re-layouts: 9.07 us -> 4.72 us
    pallas_call x1, Pallas kernels: 98.1 us -> 74.1 us  [per_device(): pl.pallas_call(kernel, out_shape=(pltpu.VMEM((D, COLS), BF16), jax.ShapeD...]
    unnamed x4, local copies, waits for them, and re-layouts: 9.07 us -> 4.72 us
where the time goes in v2:
time: 79.6 us; the launch traced here: 79.5 us
  Pallas kernels  74.1 us (93%)
  local copies, waits for them, and re-layouts  4.72 us (6%)
    pallas_call x1, Pallas kernels, per_device(): pl.pallas_call(kernel, out_shape=(pltpu.VMEM((D, COLS), BF16), jax.ShapeD...  74.1 us
    unnamed x4, local copies, waits for them, and re-layouts  4.72 us

profile of v2, /device:TPU:1, one launch (start us, length us, event | category | flops | bytes accessed | tf_op | source)
XLA Modules:
  0.0 79.5 jit_solution(17850586809273716883)
XLA Ops:
  0.6 0.0 copy-start
  0.6 0.7 copy-done
  1.3 74.1 %shard_map.50 = (bf16[2048,2048]{1,0:T(8,128)(2,1)S(1)}, f32[4,2048]{1,0:T(4,128)S(1)}) custom-call(bf16[4,2048]{1,0:T(4,128)(2,1)S(1)} %copy-done, bf16[2048,2048]{1,0:T(8,128)(2,1)} %bitcast.4, bf16[32,32768]{1,0:T(8,128)(2,1)} %bitcast.5), custom_call_target="tpu_custom_call" | custom-call | flops 12884901888 | bytes 20971520 | tf_op jit(solution)/shard_map/pallas_call | solution.py:331
  75.4 3.4 %copy.7 = bf16[1,2048,2048]{2,1,0:T(8,128)(2,1)} copy(bf16[1,2048,2048]{2,1,0:T(8,128)(2,1)S(1)} %bitcast.3) | data formatting | bytes 16777216
  78.8 0.6 copy.8
Async XLA Ops:
  0.6 0.7 copy-start

commit v3 on v2

--- a/solution.py
+++ b/solution.py
@@ -20,9 +20,11 @@
 def kernel(
     h_ref, w_hbm, t_hbm, wg_v, out_ref,
     w_v, t_v, tbuf, pack, own, st1, hs, hb, ht, e_v, lg_v,
-    col, tst_src, tstat, stx, sbuf, x0s, x0r, r1s, r1r, r2s, r2r, r3s, r3r,
+    col, tst_src, tstat, stx, sbuf, x0s, x0r,
+    a1s, a1r, a2s, a2r, a3s, a3r, b1s, b1r, b2s, b2r, r3s, r3r,
     local_sem,
-    s1, r1, sa, ra, stt, rtt, s2, r2, sf, rf, sst, rst, sx, rx, sr1, rr1, sr2, rr2, sr3, rr3,
+    s1, r1, sa, ra, stt, rtt, s2, r2, sf, rf, sst, rst, sx, rx,
+    sa1, ra1, sa2, ra2, sa3, ra3, sb1, rb1, sb2, rb2, sr3, rr3,
 ):
     hd, vc = lax.axis_index("head"), lax.axis_index("vocab")
     chip = vc // 2
@@ -44,11 +46,11 @@
     def voc_from(j):
         return lax.rem(vc + VOC - j, VOC)
 
-    def head(j):
-        return lax.rem(hd + j, HEAD)
-
-    def head_from(j):
-        return lax.rem(hd + HEAD - j, HEAD)
+    y_hi, y_lo = vc // 8, hd // 4
+    x_at = hd - 4 * y_lo
+
+    def head_at(p, j):
+        return 4 * lax.rem(y_lo + p, 2) + lax.rem(x_at + 4 + j, 4)
 
     def remote(src, dst, send, recv, **to):
         return pltpu.make_async_remote_copy(
@@ -70,51 +72,41 @@
         own[side] = pack[...].astype(BF16)
 
     barrier = pltpu.get_barrier_semaphore()
-    each(1, VOC, lambda j: pl.semaphore_signal(barrier, inc=1, device_id={"vocab": voc(j)}, device_id_type=MESH))
-    each(1, HEAD, lambda j: pl.semaphore_signal(barrier, inc=1, device_id={"head": head(j)}, device_id_type=MESH))
-    pl.semaphore_wait(barrier, VOC - 1 + HEAD - 1)
-
-    def ag1(j, owner, to):
-        return remote(own.at[lax.rem(to, 2)], st1.at[owner], s1.at[j], r1.at[j], vocab=to)
-
-    each(1, VOC, lambda j: ag1(j, vc, voc(j)).start())
-
-    y_hi = vc // 8
+
+    def greet(**to):
+        pl.semaphore_signal(barrier, inc=1, device_id=to, device_id_type=MESH)
+
+    each(1, VOC, lambda j: greet(vocab=voc(j)))
+    each(0, VOC, lambda j: greet(head=head_at(1, 0), vocab=voc(j)))
+    for p in range(2):
+        each(1, 4, lambda j: greet(head=head_at(p, j)))
+    pl.semaphore_wait(barrier, 2 * VOC - 1 + 6)
+
+    def ag1(p, j, owner, to):
+        return remote(
+            own.at[lax.rem(to, 2)], st1.at[VOC * p + owner], s1.at[VOC * p + j], r1.at[VOC * p + j],
+            head=head_at(p, 0), vocab=to,
+        )
+
+    each(1, VOC, lambda j: ag1(0, j, vc, voc(j)).start())
+    each(0, VOC, lambda j: ag1(1, j, vc, voc(j)).start())
 
     def tile_to(j):
-        near = lax.rem(vc + j, 8)
-        return 8 * lax.rem(y_hi + j // 8, 2) + near
+        return 8 * lax.rem(y_hi + j // 8, 2) + lax.rem(vc + j, 8)
 
     def tile_from(j):
-        near = lax.rem(vc + 16 - j, 8)
-        return 8 * lax.rem(y_hi + j // 8, 2) + near
+        return 8 * lax.rem(y_hi + j // 8, 2) + lax.rem(vc + 16 - j, 8)
 
     def a2a(j, owner, to):
         return remote(
             t_hbm.at[:, rows_of(to, COLS)], tbuf.at[rows_of(owner, ROWS), :], sa.at[j], ra.at[j], vocab=to
         )
 
+    each(8, VOC, lambda j: a2a(j, vc, tile_to(j)).start())
     each(1, 8, lambda j: a2a(j, vc, tile_to(j)).start())
-
-    st1[vc] = own[core]
-    each(1, VOC, lambda j: ag1(j, voc_from(j), voc(j)).wait_recv())
-    for i in range(VOC):
-        rows = st1[i].astype(F32)
-        for g in range(4):
-            hs[4 * i : 4 * i + 4, g * CW : (g + 1) * CW] = rows[4 * g : 4 * g + 4, :]
-    hb[core, rows_of(hd, HR), :] = hs[...].astype(BF16)
-
-    y_lo = hd // 4
-    x_at = hd - 4 * y_lo
-
-    def head_at(p, j):
-        return 4 * lax.rem(y_lo + p, 2) + lax.rem(x_at + 4 + j, 4)
 
     def block(side, p, j):
         return hb.at[side, rows_of(head_at(p, j), HR), :]
-
-    def agy(p):
-        return remote(block(core, p, 0), block(core, p, 0), s2.at[0], r2.at[0], head=head_at(1, 0))
 
     def agx(p, j, src):
         return remote(
@@ -125,13 +117,19 @@
         at = block(side, p, -j)
         return remote(at, at, sf.at[4 * p + j], rf.at[4 * p + j], vocab=sib)
 
-    agy(0).start()
-    each(1, 4, lambda j: agx(0, j, 0).start())
-    fwd(0, 0, core).start()
-    each(8, VOC, lambda j: a2a(j, vc, tile_to(j)).start())
-    agy(1).wait_recv()
-    each(1, 4, lambda j: agx(1, j, 0).start())
-    fwd(1, 0, core).start()
+    st1[vc] = own[core]
+    for p in range(2):
+        each(1 - p, VOC, lambda j: ag1(p, j, voc_from(j), voc(j)).wait_recv())
+        for i in range(VOC):
+            rows = st1[VOC * p + i].astype(F32)
+            for g in range(4):
+                hs[4 * i : 4 * i + 4, g * CW : (g + 1) * CW] = rows[4 * g : 4 * g + 4, :]
+        hb[core, rows_of(head_at(p, 0), HR), :] = hs[...].astype(BF16)
+        agx(p, 1, 0).start()
+        agx(p, 3, 0).start()
+        fwd(p, 0, core).start()
+    for p in range(2):
+        agx(p, 2, 0).start()
 
     t_copy.wait()
     TW = 2048
@@ -163,38 +161,48 @@
 
     each(1, VOC, lambda j: tst(j, vc).start())
 
-    for p in range(2):
-        def pass_on(j):
-            agx(p, j, -j).wait_recv()
-            fwd(p, j, core).start()
-
-        each(1, 4, pass_on)
-    for p in range(2):
-        each(0, 4, lambda j: fwd(p, j, 1 - core).wait_recv())
-    w_copy.wait()
-
-    col[0] = jnp.full((TOK, 128), -jnp.inf, F32)
-
-    def student_step(n):
-        cols = pl.ds(pl.multiple_of(n * CW, CW), CW)
-        x = jnp.dot(hb[0], w_v[:HALF, cols], preferred_element_type=F32)
-        x = x + jnp.dot(hb[1], w_v[HALF:, cols], preferred_element_type=F32)
-        e_v[n] = x
-        col[0] = jnp.maximum(col[0], jnp.maximum(x[:, :128], x[:, 128:]))
-
-    each(0, NC, student_step)
-    col[0] = jnp.broadcast_to(jnp.max(col[0], axis=1, keepdims=True), (TOK, 128))
-    col[1] = jnp.zeros((TOK, 128), F32)
-
-    def exp_step(n):
-        top_n = col[0]
-        a = jnp.exp(e_v[n, :, :128] - top_n)
-        b = jnp.exp(e_v[n, :, 128:] - top_n)
-        e_v[n, :, :128] = a
-        e_v[n, :, 128:] = b
-        col[1] = col[1] + (a + b)
-
-    each(0, NC, exp_step)
+    def student(places):
+        places = [(p, j) for j in places for p in range(2)]
+        for p, j in places:
+            if j:
+                agx(p, j, -j).wait_recv()
+                fwd(p, j, core).start()
+        for p, j in places:
+            fwd(p, j, 1 - core).wait_recv()
+        blocks = [rows_of(head_at(p, -j), HR) for p, j in places]
+        if 0 in [j for _, j in places]:
+            w_copy.wait()
+        for rows in blocks:
+            col[0, rows, :] = jnp.full((HR, 128), -jnp.inf, F32)
+            col[1, rows, :] = jnp.zeros((HR, 128), F32)
+
+        def logit_step(n):
+            cols = pl.ds(pl.multiple_of(n * CW, CW), CW)
+            low = jnp.concatenate([hb[0, rows, :] for rows in blocks])
+            x = jnp.dot(low, w_v[:HALF, cols], preferred_element_type=F32)
+            high = jnp.concatenate([hb[1, rows, :] for rows in blocks])
+            x = x + jnp.dot(high, w_v[HALF:, cols], preferred_element_type=F32)
+            for i, rows in enumerate(blocks):
+                part = x[i * HR : (i + 1) * HR]
+                e_v[n, rows, :] = part
+                col[0, rows, :] = jnp.maximum(col[0, rows, :], jnp.maximum(part[:, :128], part[:, 128:]))
+
+        each(0, NC, logit_step)
+        for rows in blocks:
+            col[0, rows, :] = jnp.broadcast_to(jnp.max(col[0, rows, :], axis=1, keepdims=True), (HR, 128))
+
+        def exp_step(n):
+            for rows in blocks:
+                a = jnp.exp(e_v[n, rows, :128] - col[0, rows, :])
+                b = jnp.exp(e_v[n, rows, 128:] - col[0, rows, :])
+                e_v[n, rows, :128] = a
+                e_v[n, rows, 128:] = b
+                col[1, rows, :] = col[1, rows, :] + (a + b)
+
+        each(0, NC, exp_step)
+
+    student((0, 1, 3))
+    student((2,))
     sums = jnp.broadcast_to(jnp.sum(col[1], axis=1, keepdims=True), (TOK, 128))
     lane_t = lax.broadcasted_iota(jnp.int32, (TOK, 128), 1)
     stats = jnp.where(lane_t == 0, col[0], sums).T[:8, :]
@@ -253,52 +261,106 @@
     def x0(k):
         return remote(x0s.at[k], x0r.at[k], sx.at[k], rx.at[k], vocab=sib)
 
-    def give_step(k):
+    def give(k):
         x0s[k] = share(1 - core, k).astype(BF16)
         x0(k).start()
 
-    each(0, DK, give_step)
-
-    def rs1(k, j, to, owner):
-        return remote(
-            r1s.at[k, to], r1r.at[k, owner], sr1.at[k * HEAD + j], rr1.at[k * HEAD + j], head=head(j)
-        )
-
-    def keep_step(k):
+    def both_cores(k):
         mine = share(core, k)
         x0(k).wait_recv()
-        r1s[k] = (mine + x0r[k].astype(F32)).astype(BF16).reshape(HEAD, HR, CW)
-        each(1, HEAD, lambda j: rs1(k, j, head(j), hd).start())
-        r1r[k, hd] = r1s[k, hd]
-
-    each(0, DK, keep_step)
+        return mine + x0r[k].astype(F32)
+
+    def chip_at(j):
+        return lax.rem(chip + CHIPS + j, CHIPS)
+
+    def a1(k, j):
+        return remote(
+            a1s.at[k, lax.rem(x_at + j, 4)], a1r.at[k, x_at], sa1.at[4 * k + j], ra1.at[4 * k + j], head=head_at(0, j)
+        )
+
+    def keep_a(k):
+        mine = both_cores(k)
+        for y in range(2):
+            for x in range(4):
+                at = (4 * y + x) * HR
+                a1s[k, x, y] = mine[at : at + HR].astype(BF16)
+        for j in (1, 3, 2):
+            a1(k, j).start()
+        a1r[k, x_at] = a1s[k, x_at]
+
+    def a2(k):
+        return remote(a2s.at[k, lax.rem(y_lo + 1, 2)], a2r.at[k], sa2.at[k], ra2.at[k], head=head_at(1, 0))
+
+    def a3(j):
+        return remote(a3s.at[chip_at(j)], a3r.at[chip], sa3.at[j], ra3.at[j], vocab=2 * chip_at(j) + core)
+
+    def b1(k, j):
+        return remote(
+            b1s.at[k, chip_at(j)], b1r.at[k, chip], sb1.at[8 * k + j], rb1.at[8 * k + j], vocab=2 * chip_at(j) + core
+        )
+
+    def keep_b(k):
+        mine = both_cores(2 + k).reshape(HEAD, CHIPS, 8, CW)
+        for q in range(CHIPS):
+            b1s[k, q] = mine[:, q].reshape(HEAD * 8, CW).astype(BF16)
+        each(1, CHIPS, lambda j: b1(k, j).start())
+        b1r[k, chip] = b1s[k, chip]
+
+    def b2(j):
+        to = lax.rem(hd + j, HEAD)
+        return remote(b2s.at[to], b2r.at[hd], sb2.at[j], rb2.at[j], head=to)
+
+    give(0)
+    give(1)
+    keep_a(0)
+    give(2)
+    keep_a(1)
+    give(3)
+    keep_b(0)
+    keep_b(1)
 
     def weight_step(n):
         rows = pl.ds(pl.multiple_of(n * CW, CW), CW)
         wg_v[rows, :] = jnp.dot(ht[rows, :], lg_v[...], preferred_element_type=F32).astype(BF16)
 
-    each(0, D // CW, weight_step)
-
-    for k in range(DK):
-        each(1, HEAD, lambda j: rs1(k, j, head(j), head_from(j)).wait_recv())
-        total = r1r[k, 0].astype(F32)
-        for i in range(1, HEAD):
-            total = total + r1r[k, i].astype(F32)
-        r2s[:, :, k * CW : (k + 1) * CW] = total.reshape(CHIPS, 8, CW)
-
-    def rs2(j, to, owner):
-        return remote(r2s.at[to], r2r.at[owner], sr2.at[j], rr2.at[j], vocab=2 * to + core)
-
-    def chip_at(j):
-        return lax.rem(chip + j, CHIPS)
-
-    each(1, CHIPS, lambda j: rs2(j, chip_at(j), chip).start())
-    r2r[chip] = r2s[chip]
-    each(1, CHIPS, lambda j: rs2(j, chip_at(j), lax.rem(chip + CHIPS - j, CHIPS)).wait_recv())
-    mine = r2r[0]
-    for i in range(1, CHIPS):
-        mine = mine + r2r[i]
-    r3s[...] = mine
+    def total_of(ref, k, count):
+        total = ref[k, 0].astype(F32)
+        for i in range(1, count):
+            total = total + ref[k, i].astype(F32)
+        return total
+
+    for k in range(2):
+        for j in (1, 3, 2):
+            a1(k, j).wait_recv()
+        a2s[k] = total_of(a1r, k, 4)
+        a2(k).start()
+
+    each(0, NC // 2, weight_step)
+
+    for k in range(2):
+        each(1, CHIPS, lambda j: b1(k, j).wait_recv())
+        b2s[:, :, k * CW : (k + 1) * CW] = total_of(b1r, k, CHIPS).reshape(HEAD, 8, CW)
+    each(1, HEAD, lambda j: b2(j).start())
+    b2r[hd] = b2s[hd]
+    for k in range(2):
+        a2(k).wait_recv()
+        a3s[:, :, k * CW : (k + 1) * CW] = (a2s[k, y_lo] + a2r[k]).reshape(CHIPS, 8, CW)
+    each(1, CHIPS, lambda j: a3(j).start())
+    a3r[chip] = a3s[chip]
+
+    each(NC // 2, NC, weight_step)
+
+    def sum_of(ref):
+        total = ref[0]
+        for i in range(1, 8):
+            total = total + ref[i]
+        return total
+
+    each(1, HEAD, lambda j: b2(j).wait_recv())
+    r3s[:, HALF // 2 :] = sum_of(b2r)
+    each(1, CHIPS, lambda j: a3(j).wait_recv())
+    r3s[:, : HALF // 2] = sum_of(a3r)
+    mine = r3s[...]
     rs3 = remote(r3s, r3r, sr3, rr3, vocab=sib)
     rs3.start()
     rs3.wait_recv()
@@ -309,18 +371,22 @@
     out_ref[:, :HALF] = jnp.where(first, low[:4], low[4:])
     out_ref[:, HALF:] = jnp.where(first, high[:4], high[4:])
 
-    each(1, VOC, lambda j: ag1(j, vc, voc(j)).wait_send())
+    for p in range(2):
+        each(1 - p, VOC, lambda j: ag1(p, j, vc, voc(j)).wait_send())
     each(1, VOC, lambda j: a2a(j, vc, tile_to(j)).wait_send())
     each(1, VOC, lambda j: tst(j, vc).wait_send())
     each(1, VOC, lambda j: st(j, vc).wait_send())
-    agy(0).wait_send()
     for p in range(2):
         each(1, 4, lambda j: agx(p, j, 0).wait_send())
         each(0, 4, lambda j: fwd(p, j, core).wait_send())
     each(0, DK, lambda k: x0(k).wait_send())
-    for k in range(DK):
-        each(1, HEAD, lambda j: rs1(k, j, head(j), hd).wait_send())
-    each(1, CHIPS, lambda j: rs2(j, chip_at(j), chip).wait_send())
+    for k in range(2):
+        for j in range(1, 4):
+            a1(k, j).wait_send()
+        a2(k).wait_send()
+        each(1, CHIPS, lambda j: b1(k, j).wait_send())
+    each(1, CHIPS, lambda j: a3(j).wait_send())
+    each(1, HEAD, lambda j: b2(j).wait_send())
     rs3.wait_send()
 
 
@@ -342,7 +408,7 @@
             pltpu.VMEM((TOK, COLS), BF16),
             pltpu.VMEM((16, CW), F32),
             pltpu.VMEM((2, 16, CW), BF16),
-            pltpu.VMEM((VOC, 16, CW), BF16),
+            pltpu.VMEM((2 * VOC, 16, CW), BF16),
             pltpu.VMEM((HR, HALF), F32),
             pltpu.VMEM((2, TOK, HALF), BF16),
             pltpu.VMEM((D, TOK), BF16),
@@ -355,17 +421,23 @@
             pltpu.VMEM((VOC, 8, 128), F32),
             pltpu.VMEM((DK, TOK, CW), BF16),
             pltpu.VMEM((DK, TOK, CW), BF16),
-            pltpu.VMEM((DK, HEAD, HR, CW), BF16),
-            pltpu.VMEM((DK, HEAD, HR, CW), BF16),
-            pltpu.VMEM((CHIPS, 8, HALF), F32),
-            pltpu.VMEM((CHIPS, 8, HALF), F32),
+            pltpu.VMEM((2, 4, 2, HR, CW), BF16),
+            pltpu.VMEM((2, 4, 2, HR, CW), BF16),
+            pltpu.VMEM((2, 2, HR, CW), F32),
+            pltpu.VMEM((2, HR, CW), F32),
+            pltpu.VMEM((CHIPS, 8, HALF // 2), F32),
+            pltpu.VMEM((CHIPS, 8, HALF // 2), F32),
+            pltpu.VMEM((2, CHIPS, HEAD * 8, CW), BF16),
+            pltpu.VMEM((2, CHIPS, HEAD * 8, CW), BF16),
+            pltpu.VMEM((HEAD, 8, HALF // 2), F32),
+            pltpu.VMEM((HEAD, 8, HALF // 2), F32),
             pltpu.VMEM((8, HALF), F32),
             pltpu.VMEM((8, HALF), F32),
             dma((3,)),
-            dma((VOC,)), dma((VOC,)), dma((VOC,)), dma((VOC,)), dma((VOC,)), dma((VOC,)),
-            dma((HEAD,)), dma((HEAD,)), dma((HEAD,)), dma((HEAD,)),
-            dma((VOC,)), dma((VOC,)), dma((DK,)), dma((DK,)),
-            dma((DK * HEAD,)), dma((DK * HEAD,)), dma((CHIPS,)), dma((CHIPS,)), dma, dma,
+            dma((2 * VOC,)), dma((2 * VOC,)), dma((VOC,)), dma((VOC,)), dma((VOC,)), dma((VOC,)),
+            dma((HEAD,)), dma((HEAD,)), dma((HEAD,)), dma((HEAD,)), dma((VOC,)), dma((VOC,)), dma((DK,)), dma((DK,)),
+            dma((8,)), dma((8,)), dma((2,)), dma((2,)), dma((CHIPS,)), dma((CHIPS,)),
+            dma((2 * CHIPS,)), dma((2 * CHIPS,)), dma((HEAD,)), dma((HEAD,)), dma, dma,
         ],
         compiler_params=pltpu.CompilerParams(
             collective_id=0, has_side_effects=True, vmem_limit_bytes=44 * 1024 * 1024

time: 79.6 us -> 77.4 us (0.972)
  Pallas kernels: 74.1 us -> 71.9 us
    pallas_call x1, Pallas kernels: 74.1 us -> 71.9 us  [per_device(): pl.pallas_call(kernel, out_shape=(pltpu.VMEM((D, COLS), BF16), jax.ShapeD...]
where the time goes in v3:
time: 77.4 us; the launch traced here: 77.2 us
  Pallas kernels  71.9 us (93%)
  local copies, waits for them, and re-layouts  4.72 us (6%)
    pallas_call x1, Pallas kernels, per_device(): pl.pallas_call(kernel, out_shape=(pltpu.VMEM((D, COLS), BF16), jax.ShapeD...  71.9 us
    unnamed x4, local copies, waits for them, and re-layouts  4.72 us

profile of v3, /device:TPU:1, one launch (start us, length us, event | category | flops | bytes accessed | tf_op | source)
XLA Modules:
  0.0 77.2 jit_solution(852428744254723590)
XLA Ops:
  0.6 0.0 copy-start
  0.6 0.7 copy-done
  1.3 71.9 %shard_map.50 = (bf16[2048,2048]{1,0:T(8,128)(2,1)S(1)}, f32[4,2048]{1,0:T(4,128)S(1)}) custom-call(bf16[4,2048]{1,0:T(4,128)(2,1)S(1)} %copy-done, bf16[2048,2048]{1,0:T(8,128)(2,1)} %bitcast.4, bf16[32,32768]{1,0:T(8,128)(2,1)} %bitcast.5), custom_call_target="tpu_custom_call" | custom-call | flops 12884901888 | bytes 20971520 | tf_op jit(solution)/shard_map/pallas_call | solution.py:397
  73.2 3.4 %copy.7 = bf16[1,2048,2048]{2,1,0:T(8,128)(2,1)} copy(bf16[1,2048,2048]{2,1,0:T(8,128)(2,1)S(1)} %bitcast.3) | data formatting | bytes 16777216
  76.6 0.6 copy.8
Async XLA Ops:
  0.6 0.7 copy-start

commit v4 on v2

v4 whole, which is shorter than its diff:
```python
import jax
import jax.numpy as jnp
from jax import lax
from jax.experimental import pallas as pl
from jax.experimental.pallas import tpu as pltpu
from jax.sharding import PartitionSpec as P

MESH = pl.DeviceIdType.MESH
F32, BF16 = jnp.float32, jnp.bfloat16
HEAD, VOC, CHIPS = 8, 16, 8
D, TOK, COLS = 2048, 512, 2048
ROWS = TOK // VOC
HR = TOK // HEAD
HALF = D // 2
CW = 256
NC = COLS // CW
BW = 512
NB = COLS // BW
GR = TOK // 2
WG_FIRST = 3
DK = HALF // BW


def kernel(
    h_ref, w_hbm, t_hbm, wg_v, out_ref,
    w_v, t_v, tbuf, pack, own, st1, hs, hb, ht, e_v, lg_v,
    col, tcol, tst_src, tstat, stx, sbuf, x0s, x0r,
    a1s, a1r, a2s, a2r, b1s, b1r, b2s, b2r, r3s, r3r,
    local_sem,
    s1, r1, sa, ra, stt, rtt, s2, r2, sf, rf, sst, rst, sx, rx,
    sa1, ra1, sa2, ra2, sb1, rb1, sb2, rb2, sr3, rr3,
):
    hd, vc = lax.axis_index("head"), lax.axis_index("vocab")
    chip = vc // 2
    core = vc - 2 * chip
    sib = 2 * chip + 1 - core

    def rows_of(index, count):
        return pl.ds(pl.multiple_of(index * count, count), count)

    def each(start, stop, body):
        def step(j, carry):
            body(j)
            return carry
        lax.fori_loop(start, stop, step, 0)

    def voc(j):
        return lax.rem(vc + j, VOC)

    def voc_from(j):
        return lax.rem(vc + VOC - j, VOC)

    y_hi, y_lo = vc // 8, hd // 4
    x_at = hd - 4 * y_lo

    def y_of(group):
        return lax.rem(y_hi + group, 2)

    def head_at(group, j):
        return 4 * y_of(group) + lax.rem(x_at + 4 + j, 4)

    def beside(p):
        return 4 * lax.rem(y_lo + p, 2) + x_at

    def along_x(j):
        return 4 * y_lo + lax.rem(x_at + j, 4)

    def remote(src, dst, send, recv, **to):
        return pltpu.make_async_remote_copy(
            src_ref=src, dst_ref=dst, send_sem=send, recv_sem=recv, device_id=to, device_id_type=MESH
        )

    w_copy = pltpu.make_async_copy(w_hbm, w_v, local_sem.at[0])
    t_copy = pltpu.make_async_copy(t_hbm, t_v, local_sem.at[1])
    own_tile = pltpu.make_async_copy(
        t_hbm.at[:, rows_of(vc, COLS)], tbuf.at[rows_of(vc, ROWS), :], local_sem.at[2]
    )
    t_copy.start()
    w_copy.start()
    own_tile.start()
    for side in range(2):
        for g in range(4):
            at = side * HALF + g * CW
            pack[4 * g : 4 * g + 4, :] = h_ref[:, at : at + CW].astype(F32)
        own[side] = pack[...].astype(BF16)

    barrier = pltpu.get_barrier_semaphore()

    def greet(**to):
        pl.semaphore_signal(barrier, inc=1, device_id=to, device_id_type=MESH)

    each(1, VOC, lambda j: greet(vocab=voc(j)))
    each(0, VOC, lambda j: greet(head=beside(1), vocab=voc(j)))
    each(1, 4, lambda j: greet(head=along_x(j)))
    each(1, 4, lambda j: greet(head=4 * lax.rem(y_lo + 1, 2) + lax.rem(x_at + j, 4)))
    pl.semaphore_wait(barrier, 2 * VOC - 1 + 6)

    def ag1(p, j, owner, to):
        return remote(
            own.at[lax.rem(to, 2)], st1.at[owner], s1.at[VOC * p + j], r1.at[VOC * p + j],
            head=beside(p), vocab=to,
        )

    each(1, VOC, lambda j: ag1(0, j, VOC * y_lo + vc, voc(j)).start())
    each(0, VOC, lambda j: ag1(1, j, VOC * y_lo + vc, voc(j)).start())

    def tile_to(j):
        return 8 * lax.rem(y_hi + j // 8, 2) + lax.rem(vc + j, 8)

    def tile_from(j):
        return 8 * lax.rem(y_hi + j // 8, 2) + lax.rem(vc + 16 - j, 8)

    def a2a(j, owner, to):
        return remote(
            t_hbm.at[:, rows_of(to, COLS)], tbuf.at[rows_of(owner, ROWS), :], sa.at[j], ra.at[j], vocab=to
        )

    each(8, VOC, lambda j: a2a(j, vc, tile_to(j)).start())
    each(1, 8, lambda j: a2a(j, vc, tile_to(j)).start())

    def block(side, p, j):
        return hb.at[side, rows_of(head_at(p, j), HR), :]

    def agx(p, j, src):
        return remote(
            block(core, p, src), block(core, p, src), s2.at[4 * p + j], r2.at[4 * p + j], head=along_x(j)
        )

    def fwd(p, j, side):
        at = block(side, p, -j)
        return remote(at, at, sf.at[4 * p + j], rf.at[4 * p + j], vocab=sib)

    t_copy.wait()
    TW = 2048

    def top_step(i, top):
        x = t_v[:, pl.ds(pl.multiple_of(i * TW, TW), TW)].astype(F32)
        for k in range(TW // 128):
            top = jnp.maximum(top, x[:, k * 128 : (k + 1) * 128])
        return top

    top = lax.fori_loop(0, COLS * VOC // TW, top_step, jnp.full((ROWS, 128), -jnp.inf, F32))
    top = jnp.broadcast_to(jnp.max(top, axis=1, keepdims=True), (ROWS, 128))

    def sum_step(i, total):
        x = t_v[:, pl.ds(pl.multiple_of(i * TW, TW), TW)].astype(F32)
        for k in range(TW // 128):
            total = total + jnp.exp(x[:, k * 128 : (k + 1) * 128] - top)
        return total

    total = lax.fori_loop(0, COLS * VOC // TW, sum_step, jnp.zeros((ROWS, 128), F32))
    scale = 1.0 / jnp.broadcast_to(jnp.sum(total, axis=1, keepdims=True), (ROWS, 128))
    lane = lax.broadcasted_iota(jnp.int32, (ROWS, 128), 1)
    both = jnp.concatenate([jnp.where(lane == 0, top, scale), jnp.zeros((128 - ROWS, 128), F32)])
    tst_src[...] = both.T[:8]
    tstat[vc] = tst_src[...]

    def tst(j, owner):
        return remote(tst_src, tstat.at[owner], stt.at[j], rtt.at[j], vocab=voc(j))

    each(1, VOC, lambda j: tst(j, vc).start())

    st1[VOC * y_lo + vc] = own[core]
    for p in range(2):
        each(1 - p, VOC, lambda j: ag1(p, j, VOC * lax.rem(y_lo + p, 2) + voc_from(j), voc(j)).wait_recv())
    for group in range(2):
        for i in range(VOC):
            rows = st1[VOC * y_of(group) + i].astype(F32)
            for g in range(4):
                hs[4 * i : 4 * i + 4, g * CW : (g + 1) * CW] = rows[4 * g : 4 * g + 4, :]
        hb[core, rows_of(head_at(group, 0), HR), :] = hs[...].astype(BF16)
        if group == 0:
            for j in (1, 3, 2):
                agx(0, j, 0).start()
        fwd(group, 0, core).start()

    def group_rows(group):
        return rows_of(y_of(group), GR)

    def st(group, j, owner):
        at = VOC * y_of(group) + j
        return remote(stx.at[group], sbuf.at[y_of(group), owner], sst.at[at], rst.at[at], vocab=voc(j))

    def student(group):
        rows = group_rows(group)
        if group == 0:
            each(1, 4, lambda j: agx(0, j, 0).wait_send())
            for j in (1, 3, 2):
                agx(1, j, 0).start()
        for j in (1, 3, 2):
            agx(group, j, -j).wait_recv()
            fwd(group, j, core).start()
        each(0, 4, lambda j: fwd(group, j, 1 - core).wait_recv())
        if group == 0:
            w_copy.wait()
        col[0] = jnp.full((GR, 128), -jnp.inf, F32)
        col[1] = jnp.zeros((GR, 128), F32)

        def logit_step(n):
            cols = pl.ds(pl.multiple_of(n * BW, BW), BW)
            x = jnp.dot(hb[0, rows, :], w_v[:HALF, cols], preferred_element_type=F32)
            x = x + jnp.dot(hb[1, rows, :], w_v[HALF:, cols], preferred_element_type=F32)
            e_v[n, rows, :] = x
            top_n = col[0]
            for i in range(BW // 128):
                top_n = jnp.maximum(top_n, x[:, i * 128 : (i + 1) * 128])
            col[0] = top_n

        each(0, NB, logit_step)
        col[0] = jnp.broadcast_to(jnp.max(col[0], axis=1, keepdims=True), (GR, 128))

        def exp_step(n):
            total_n = col[1]
            for i in range(BW // 128):
                a = jnp.exp(e_v[n, rows, i * 128 : (i + 1) * 128] - col[0])
                e_v[n, rows, i * 128 : (i + 1) * 128] = a
                total_n = total_n + a
            col[1] = total_n

        each(0, NB, exp_step)
        sums = jnp.broadcast_to(jnp.sum(col[1], axis=1, keepdims=True), (GR, 128))
        lane_t = lax.broadcasted_iota(jnp.int32, (GR, 128), 1)
        stats = jnp.where(lane_t == 0, col[0], sums).T[:8, :]
        for i in range(2):
            stx[group, i : i + 1, :] = stats[0:1, i * 128 : (i + 1) * 128]
            stx[group, 2 + i : 3 + i, :] = stats[1:2, i * 128 : (i + 1) * 128]
        stx[group, 4:, :] = jnp.zeros((4, 128), F32)
        sbuf[y_of(group), vc] = stx[group]
        each(1, VOC, lambda j: st(group, j, vc).start())

    def transposed_trunk(group):
        rows = group_rows(group)
        for half in range(2):
            for k in range(HALF // CW):
                ht[half * HALF + k * CW : half * HALF + (k + 1) * CW, rows] = (
                    hb[half, rows, k * CW : (k + 1) * CW].T
                )

    student(0)
    transposed_trunk(0)
    student(1)

    each(1, VOC, lambda j: tst(j, voc_from(j)).wait_recv())
    for i in range(4):
        rows = jnp.concatenate([tstat[4 * i + k][:, :ROWS] for k in range(4)], axis=1)
        rows = jnp.concatenate([rows, jnp.zeros((120, 128), F32)]).T
        tcol[0, i * 128 : (i + 1) * 128, :] = jnp.broadcast_to(rows[:, 0:1], (128, 128))
        tcol[1, i * 128 : (i + 1) * 128, :] = jnp.broadcast_to(rows[:, 1:2], (128, 128))

    def grad(group):
        rows = group_rows(group)
        each(1, VOC, lambda j: st(group, j, voc_from(j)).wait_recv())
        tops = [sbuf[y_of(group), i][:2] for i in range(VOC)]
        parts = [sbuf[y_of(group), i][2:4] for i in range(VOC)]
        top_all = tops[0]
        for x in tops[1:]:
            top_all = jnp.maximum(top_all, x)
        total_all = jnp.zeros_like(top_all)
        for x, y in zip(tops, parts):
            total_all = total_all + y * jnp.exp(x - top_all)
        factor = jnp.exp(stx[group][:2] - top_all) / total_all
        for i in range(2):
            col[0, i * 128 : (i + 1) * 128, :] = jnp.broadcast_to(factor[i : i + 1], (128, 128)).T
        if group == 0:
            own_tile.wait()
        near = 8 * group
        each(max(near, 1), near + 8, lambda j: a2a(j, tile_from(j), tile_to(j)).wait_recv())

        def grad_step(n):
            for side in range(BW // 128):
                cols = pl.ds(pl.multiple_of(n * BW + side * 128, 128), 128)
                teacher = jnp.exp(tbuf[rows, cols].astype(F32) - tcol[0, rows, :]) * tcol[1, rows, :]
                student = e_v[n, rows, side * 128 : side * 128 + 128] * col[0]
                lg_v[rows, cols] = (student - teacher).astype(BF16)

        each(0, NB, grad_step)

    def share(group, half, k):
        at = pl.ds(pl.multiple_of(half * HALF + k * BW, BW), BW)
        return lax.dot_general(
            lg_v[group_rows(group), :], w_v[at, :], (((1,), (1,)), ((), ())), preferred_element_type=F32
        )

    def x0(group, k):
        at = DK * group + k
        return remote(x0s.at[at], x0r.at[at], sx.at[at], rx.at[at], vocab=sib)

    def a1(group, j):
        at = 4 * group + j
        return remote(
            a1s.at[group, lax.rem(x_at + j, 4)], a1r.at[group, x_at], sa1.at[at], ra1.at[at], head=along_x(j)
        )

    def b1(y, j, src):
        at = CHIPS * y + j
        return remote(
            b1s.at[src, chip_at(j)], b1r.at[y, chip], sb1.at[at], rb1.at[at], vocab=2 * chip_at(j) + core
        )

    def b2(j):
        to = lax.rem(hd + j, HEAD)
        return remote(b2s.at[to], b2r.at[hd], sb2.at[j], rb2.at[j], head=to)

    def chip_at(j):
        return lax.rem(chip + CHIPS + j, CHIPS)

    def give(group, k):
        x0s[DK * group + k] = share(group, 1 - core, k).astype(BF16)
        x0(group, k).start()

    def both_cores(group, k):
        at = DK * group + k
        mine = share(group, core, k)
        x0(group, k).wait_recv()
        return mine + x0r[at].astype(F32)

    def shares(group):
        give(group, 0)
        give(group, 1)
        mine = both_cores(group, 0)
        for x in range(4):
            a1s[group, x] = mine[x * HR : (x + 1) * HR].astype(BF16)
        for j in (2, 1, 3):
            a1(group, j).start()
        a1r[group, x_at] = a1s[group, x_at]
        mine = both_cores(group, 1).reshape(4, CHIPS, 8, BW)
        for q in range(CHIPS):
            b1s[group, q] = mine[:, q].reshape(32, BW).astype(BF16)
        each(1, CHIPS, lambda j: b1(y_of(group), j, group).start())
        b1r[y_of(group), chip] = b1s[group, chip]

    def a2(group, p, j, owner_y, owner_chip):
        at = CHIPS * p + j
        return remote(
            a2s.at[group, chip_at(j)], a2r.at[owner_y, owner_chip], sa2.at[at], ra2.at[at],
            head=beside(p), vocab=2 * chip_at(j) + core,
        )

    def pass_sums(group):
        for j in range(1, 4):
            a1(group, j).wait_recv()
        total = a1r[group, 0].astype(F32)
        for x in range(1, 4):
            total = total + a1r[group, x].astype(F32)
        a2s[group] = total.reshape(CHIPS, 8, BW)
        p = lax.rem(y_of(group) + y_lo, 2)
        each(1, CHIPS, lambda j: a2(group, p, j, y_lo, chip).start())

        @pl.when(p == 1)
        def _():
            a2(group, p, 0, y_lo, chip).start()

        @pl.when(p == 0)
        def _():
            a2r[y_lo, chip] = a2s[group, chip]

    def pass_other_sums():
        for y in range(2):
            each(1, CHIPS, lambda j: b1(y, j, 0).wait_recv())
            total = b1r[y, 0].astype(F32)
            for q in range(1, CHIPS):
                total = total + b1r[y, q].astype(F32)
            b2s[4 * y : 4 * y + 4] = total.reshape(4, 8, BW)
        each(1, HEAD, lambda j: b2(j).start())
        b2r[hd] = b2s[hd]

    def weight_step(n):
        rows = pl.ds(pl.multiple_of(n * CW, CW), CW)
        wg_v[rows, :] = jnp.dot(ht[rows, :], lg_v[...], preferred_element_type=F32).astype(BF16)

    grad(0)
    shares(0)
    grad(1)
    shares(1)
    pass_sums(0)
    transposed_trunk(1)
    each(0, WG_FIRST, weight_step)
    pass_sums(1)
    pass_other_sums()
    each(WG_FIRST, NC, weight_step)

    for p in range(2):
        each(1 - p, CHIPS, lambda j: a2(0, p, j, lax.rem(y_lo + p, 2), chip_at(-j)).wait_recv())
    total = jnp.zeros((8, BW), F32)
    for p in range(2):
        for q in range(CHIPS):
            total = total + a2r[p, q]
    r3s[:, :BW] = total
    each(1, HEAD, lambda j: b2(j).wait_recv())
    total = b2r[0]
    for i in range(1, HEAD):
        total = total + b2r[i]
    r3s[:, BW:] = total
    mine = r3s[...]
    rs3 = remote(r3s, r3r, sr3, rr3, vocab=sib)
    rs3.start()
    rs3.wait_recv()
    other = r3r[...]
    first = core == 0
    low = jnp.where(first, mine, other)
    high = jnp.where(first, other, mine)
    out_ref[:, :HALF] = jnp.where(first, low[:4], low[4:])
    out_ref[:, HALF:] = jnp.where(first, high[:4], high[4:])

    for p in range(2):
        each(1 - p, VOC, lambda j: ag1(p, j, VOC * y_lo + vc, voc(j)).wait_send())
    each(1, VOC, lambda j: a2a(j, vc, tile_to(j)).wait_send())
    each(1, VOC, lambda j: tst(j, vc).wait_send())
    for group in range(2):
        each(1, VOC, lambda j: st(group, j, vc).wait_send())
    each(1, 4, lambda j: agx(1, j, 0).wait_send())
    for p in range(2):
        each(0, 4, lambda j: fwd(p, j, core).wait_send())
    for group in range(2):
        each(0, DK, lambda k: x0(group, k).wait_send())
        each(1, 4, lambda j: a1(group, j).wait_send())
        each(1, CHIPS, lambda j: b1(group, j, 0).wait_send())
    each(1, HEAD, lambda j: b2(j).wait_send())
    for p in range(2):
        each(1 - p, CHIPS, lambda j: a2(0, p, j, y_lo, chip).wait_send())
    rs3.wait_send()


def per_device(hidden_rows, head_weight, teacher_logits):
    hbm = pl.BlockSpec(memory_space=pltpu.MemorySpace.HBM)
    vmem = pl.BlockSpec(memory_space=pltpu.VMEM)
    dma = pltpu.SemaphoreType.DMA
    weight_grad, input_grad = pl.pallas_call(
        kernel,
        out_shape=(
            pltpu.VMEM((D, COLS), BF16),
            jax.ShapeDtypeStruct((TOK // (HEAD * VOC), D), F32),
        ),
        in_specs=[vmem, hbm, hbm],
        out_specs=(vmem, vmem),
        scratch_shapes=[
            pltpu.VMEM((D, COLS), BF16),
            pltpu.VMEM((ROWS, COLS * VOC), BF16),
            pltpu.VMEM((TOK, COLS), BF16),
            pltpu.VMEM((16, CW), F32),
            pltpu.VMEM((2, 16, CW), BF16),
            pltpu.VMEM((2 * VOC, 16, CW), BF16),
            pltpu.VMEM((HR, HALF), F32),
            pltpu.VMEM((2, TOK, HALF), BF16),
            pltpu.VMEM((D, TOK), BF16),
            pltpu.VMEM((NB, TOK, BW), F32),
            pltpu.VMEM((TOK, COLS), BF16),
            pltpu.VMEM((2, GR, 128), F32),
            pltpu.VMEM((2, TOK, 128), F32),
            pltpu.VMEM((8, 128), F32),
            pltpu.VMEM((VOC, 8, 128), F32),
            pltpu.VMEM((2, 8, 128), F32),
            pltpu.VMEM((2, VOC, 8, 128), F32),
            pltpu.VMEM((2 * DK, GR, BW), BF16),
            pltpu.VMEM((2 * DK, GR, BW), BF16),
            pltpu.VMEM((2, 4, HR, BW), BF16),
            pltpu.VMEM((2, 4, HR, BW), BF16),
            pltpu.VMEM((2, CHIPS, 8, BW), F32),
            pltpu.VMEM((2, CHIPS, 8, BW), F32),
            pltpu.VMEM((2, CHIPS, 32, BW), BF16),
            pltpu.VMEM((2, CHIPS, 32, BW), BF16),
            pltpu.VMEM((HEAD, 8, BW), F32),
            pltpu.VMEM((HEAD, 8, BW), F32),
            pltpu.VMEM((8, HALF), F32),
            pltpu.VMEM((8, HALF), F32),
            dma((3,)),
            dma((2 * VOC,)), dma((2 * VOC,)), dma((VOC,)), dma((VOC,)), dma((VOC,)), dma((VOC,)),
            dma((8,)), dma((8,)), dma((8,)), dma((8,)),
            dma((2 * VOC,)), dma((2 * VOC,)), dma((2 * DK,)), dma((2 * DK,)),
            dma((8,)), dma((8,)), dma((2 * CHIPS,)), dma((2 * CHIPS,)),
            dma((2 * CHIPS,)), dma((2 * CHIPS,)), dma((HEAD,)), dma((HEAD,)), dma, dma,
        ],
        compiler_params=pltpu.CompilerParams(
            collective_id=0, has_side_effects=True, vmem_limit_bytes=44 * 1024 * 1024
        ),
        cost_estimate=pl.CostEstimate(
            flops=6 * TOK * D * COLS, bytes_accessed=20 * 1024 * 1024, transcendentals=3 * TOK * COLS
        ),
    )(hidden_rows, head_weight[0], teacher_logits[0])
    return weight_grad[None], input_grad


def solution(mesh):
    return jax.shard_map(
        per_device,
        mesh=mesh,
        in_specs=(P(("head", "vocab"), None), P("head", None, "vocab"), P("head", "vocab", None)),
        out_specs=(P("head", None, "vocab"), P(("head", "vocab"), None)),
        check_vma=False,
    )
```

time: 79.6 us -> 71.7 us (0.901)
  Pallas kernels: 74.1 us -> 66.1 us
    pallas_call x1, Pallas kernels: 74.1 us -> 66.1 us  [per_device(): pl.pallas_call(kernel, out_shape=(pltpu.VMEM((D, COLS), BF16), jax.ShapeD...]
where the time goes in v4:
time: 71.7 us; the launch traced here: 71.5 us
  Pallas kernels  66.1 us (92%)
  local copies, waits for them, and re-layouts  4.72 us (7%)
    pallas_call x1, Pallas kernels, per_device(): pl.pallas_call(kernel, out_shape=(pltpu.VMEM((D, COLS), BF16), jax.ShapeD...  66.1 us
    unnamed x4, local copies, waits for them, and re-layouts  4.72 us

profile of v4, /device:TPU:1, one launch (start us, length us, event | category | flops | bytes accessed | tf_op | source)
XLA Modules:
  0.0 71.5 jit_solution(9731760422281195447)
XLA Ops:
  0.6 0.0 copy-start
  0.6 0.7 copy-done
  1.3 66.1 %shard_map.50 = (bf16[2048,2048]{1,0:T(8,128)(2,1)S(1)}, f32[4,2048]{1,0:T(4,128)S(1)}) custom-call(bf16[4,2048]{1,0:T(4,128)(2,1)S(1)} %copy-done, bf16[2048,2048]{1,0:T(8,128)(2,1)} %bitcast.4, bf16[32,32768]{1,0:T(8,128)(2,1)} %bitcast.5), custom_call_target="tpu_custom_call" | custom-call | flops 12884901888 | bytes 20971520 | tf_op jit(solution)/shard_map/pallas_call | solution.py:428
  67.5 3.4 %copy.7 = bf16[1,2048,2048]{2,1,0:T(8,128)(2,1)} copy(bf16[1,2048,2048]{2,1,0:T(8,128)(2,1)S(1)} %bitcast.3) | data formatting | bytes 16777216
  70.9 0.6 copy.8
Async XLA Ops:
  0.6 0.7 %copy-start = (bf16[4,2048]{1,0:T(4,128)(2,1)S(1)}, bf16[4,2048]{1,0:T(4,128)(2,1)}, u32[]{:S(2)}) copy-start(bf16[4,2048]{1,0:T(4,128)(2,1)} %h_ref.1) | copy-start | bytes 49156

commit v5 on v4

--- a/solution.py
+++ b/solution.py
@@ -22,8 +22,8 @@
 
 
 def kernel(
-    h_ref, w_hbm, t_hbm, wg_v, out_ref,
-    w_v, t_v, tbuf, pack, own, st1, hs, hb, ht, e_v, lg_v,
+    h_hbm, w_hbm, t_hbm, wg_v, out_ref,
+    h_v, w_v, t_v, tbuf, pack, own, st1, hs, hb, ht, e_v, lg_v,
     col, tcol, tst_src, tstat, stx, sbuf, x0s, x0r,
     a1s, a1r, a2s, a2r, b1s, b1r, b2s, b2r, r3s, r3r,
     local_sem,
@@ -75,15 +75,11 @@
     own_tile = pltpu.make_async_copy(
         t_hbm.at[:, rows_of(vc, COLS)], tbuf.at[rows_of(vc, ROWS), :], local_sem.at[2]
     )
+    h_copy = pltpu.make_async_copy(h_hbm, h_v, local_sem.at[3])
+    h_copy.start()
     t_copy.start()
     w_copy.start()
     own_tile.start()
-    for side in range(2):
-        for g in range(4):
-            at = side * HALF + g * CW
-            pack[4 * g : 4 * g + 4, :] = h_ref[:, at : at + CW].astype(F32)
-        own[side] = pack[...].astype(BF16)
-
     barrier = pltpu.get_barrier_semaphore()
 
     def greet(**to):
@@ -93,6 +89,12 @@
     each(0, VOC, lambda j: greet(head=beside(1), vocab=voc(j)))
     each(1, 4, lambda j: greet(head=along_x(j)))
     each(1, 4, lambda j: greet(head=4 * lax.rem(y_lo + 1, 2) + lax.rem(x_at + j, 4)))
+    h_copy.wait()
+    for side in range(2):
+        for g in range(4):
+            at = side * HALF + g * CW
+            pack[4 * g : 4 * g + 4, :] = h_v[:, at : at + CW].astype(F32)
+        own[side] = pack[...].astype(BF16)
     pl.semaphore_wait(barrier, 2 * VOC - 1 + 6)
 
     def ag1(p, j, owner, to):
@@ -371,8 +373,8 @@
     grad(0)
     shares(0)
     grad(1)
+    pass_sums(0)
     shares(1)
-    pass_sums(0)
     transposed_trunk(1)
     each(0, WG_FIRST, weight_step)
     pass_sums(1)
@@ -431,9 +433,10 @@
             pltpu.VMEM((D, COLS), BF16),
             jax.ShapeDtypeStruct((TOK // (HEAD * VOC), D), F32),
         ),
-        in_specs=[vmem, hbm, hbm],
+        in_specs=[hbm, hbm, hbm],
         out_specs=(vmem, vmem),
         scratch_shapes=[
+            pltpu.VMEM((TOK // (HEAD * VOC), D), BF16),
             pltpu.VMEM((D, COLS), BF16),
             pltpu.VMEM((ROWS, COLS * VOC), BF16),
             pltpu.VMEM((TOK, COLS), BF16),
@@ -463,7 +466,7 @@
             pltpu.VMEM((HEAD, 8, BW), F32),
             pltpu.VMEM((8, HALF), F32),
             pltpu.VMEM((8, HALF), F32),
-            dma((3,)),
+            dma((4,)),
             dma((2 * VOC,)), dma((2 * VOC,)), dma((VOC,)), dma((VOC,)), dma((VOC,)), dma((VOC,)),
             dma((8,)), dma((8,)), dma((8,)), dma((8,)),
             dma((2 * VOC,)), dma((2 * VOC,)), dma((2 * DK,)), dma((2 * DK,)),

time: 71.7 us -> 74 us (1.032)
  Pallas kernels: 66.1 us -> 68.4 us
    pallas_call x1, Pallas kernels: 66.1 us -> 68.4 us  [per_device(): pl.pallas_call(kernel, out_shape=(pltpu.VMEM((D, COLS), BF16), jax.ShapeD...]
where the time goes in v5:
time: 74 us; the launch traced here: 73.8 us
  Pallas kernels  68.4 us (92%)
  local copies, waits for them, and re-layouts  4.72 us (6%)
    pallas_call x1, Pallas kernels, per_device(): pl.pallas_call(kernel, out_shape=(pltpu.VMEM((D, COLS), BF16), jax.ShapeD...  68.4 us
    unnamed x4, local copies, waits for them, and re-layouts  4.72 us

profile of v5, /device:TPU:1, one launch (start us, length us, event | category | flops | bytes accessed | tf_op | source)
XLA Modules:
  0.0 73.8 jit_solution(9306140045321780228)
XLA Ops:
  0.6 0.0 copy-start
  0.6 0.7 copy-done
  1.3 68.4 %shard_map.50 = (bf16[2048,2048]{1,0:T(8,128)(2,1)S(1)}, f32[4,2048]{1,0:T(4,128)S(1)}) custom-call(bf16[4,2048]{1,0:T(4,128)(2,1)S(1)} %copy-done, bf16[2048,2048]{1,0:T(8,128)(2,1)} %bitcast.4, bf16[32,32768]{1,0:T(8,128)(2,1)} %bitcast.5), custom_call_target="tpu_custom_call" | custom-call | flops 12884901888 | bytes 20971520 | tf_op jit(solution)/shard_map/pallas_call | solution.py:430
  69.8 3.4 %copy.7 = bf16[1,2048,2048]{2,1,0:T(8,128)(2,1)} copy(bf16[1,2048,2048]{2,1,0:T(8,128)(2,1)S(1)} %bitcast.3) | data formatting | bytes 16777216
  73.2 0.6 copy.8
Async XLA Ops:
  0.6 0.7 copy-start

commit v6 on v5

--- a/solution.py
+++ b/solution.py
@@ -373,8 +373,8 @@
     grad(0)
     shares(0)
     grad(1)
+    shares(1)
     pass_sums(0)
-    shares(1)
     transposed_trunk(1)
     each(0, WG_FIRST, weight_step)
     pass_sums(1)

time: 74 us -> 71.4 us (0.965)
  Pallas kernels: 68.4 us -> 65.8 us
    pallas_call x1, Pallas kernels: 68.4 us -> 65.8 us  [per_device(): pl.pallas_call(kernel, out_shape=(pltpu.VMEM((D, COLS), BF16), jax.ShapeD...]
where the time goes in v6:
time: 71.4 us; the launch traced here: 71.2 us
  Pallas kernels  65.8 us (92%)
  local copies, waits for them, and re-layouts  4.72 us (7%)
    pallas_call x1, Pallas kernels, per_device(): pl.pallas_call(kernel, out_shape=(pltpu.VMEM((D, COLS), BF16), jax.ShapeD...  65.8 us
    unnamed x4, local copies, waits for them, and re-layouts  4.72 us

profile of v6, /device:TPU:1, one launch (start us, length us, event | category | flops | bytes accessed | tf_op | source)
XLA Modules:
  0.0 71.2 jit_solution(12162187092932824501)
XLA Ops:
  0.6 0.0 copy-start
  0.6 0.7 copy-done
  1.3 65.8 %shard_map.50 = (bf16[2048,2048]{1,0:T(8,128)(2,1)S(1)}, f32[4,2048]{1,0:T(4,128)S(1)}) custom-call(bf16[4,2048]{1,0:T(4,128)(2,1)S(1)} %copy-done, bf16[2048,2048]{1,0:T(8,128)(2,1)} %bitcast.4, bf16[32,32768]{1,0:T(8,128)(2,1)} %bitcast.5), custom_call_target="tpu_custom_call" | custom-call | flops 12884901888 | bytes 20971520 | tf_op jit(solution)/shard_map/pallas_call | solution.py:430
  67.2 3.4 %copy.7 = bf16[1,2048,2048]{2,1,0:T(8,128)(2,1)} copy(bf16[1,2048,2048]{2,1,0:T(8,128)(2,1)S(1)} %bitcast.3) | data formatting | bytes 16777216
  70.6 0.6 copy.8
Async XLA Ops:
  0.6 0.7 %copy-start = (bf16[4,2048]{1,0:T(4,128)(2,1)S(1)}, bf16[4,2048]{1,0:T(4,128)(2,1)}, u32[]{:S(2)}) copy-start(bf16[4,2048]{1,0:T(4,128)(2,1)} %h_hbm.1) | copy-start | bytes 49156
